TPU v7x, 32 devices: a whole 2x2x4 slice. The times are simulated.
32 devices in a mesh: tile: 8 (over z, y), slab: 4 (over x, core).
Axes of the slice: x: 2, y: 2, z: 4, core: 2. Of those that a mesh axis runs over, the one named last changes fastest.
Arguments:
- volume: bfloat16 [8, 64, 64, 256], P('tile', 'slab'), may hold values from -24 to 24
- partner: int32 [8], replicated, may hold values from 0 to 7, as said below
- offsets: int32 [8], replicated, may hold values from 0 to 7
- starts: int32 [512], P(('tile', 'slab')), may hold values from 0 to 192
- classifier: int32 [512, 1], P(('tile', 'slab')), may hold values from 0 to 7; in each aligned block of 16 rows (0 to 15, 16 to 31, ...) at most 2 rows name the same one
- stem_weight: bfloat16 [8, 512, 256], P('tile'), may hold values from -0.25 to 0.25
- expand_weight: bfloat16 [8, 1, 256, 1024], P('tile'), may hold values from -0.375 to 0.375
- shrink_weight: bfloat16 [8, 1, 1024, 256], P('tile'), may hold values from -0.1875 to 0.1875
- head_weight: bfloat16 [8, 256, 8], P('tile'), may hold values from -0.375 to 0.375
Outputs:
- log_response: float32 [8, 64, 64, 256], P('tile', 'slab')
- logits: float32 [512, 8], P(('tile', 'slab'))
Inputs may be any that keep to these rules, and one draw needn't show every extreme that they name: partner[partner[t]] = t and partner[t] != t for every tile t. Among the 16 candidates of one device at most 2 name the same classifier.
All inputs are finite; a program needn't handle non-finite values.
Results may differ from a plain program's by a relative error of at most 0.0024.
Values may be sent and summed in bfloat16 or wider, within the bound.
A program may use at most 320 MiB of HBM per device.

v0:
```python
import math

import jax
import jax.numpy as jnp
from jax import lax
from jax.sharding import PartitionSpec as P

OV = 32
CX = 64
CAP = 2


RADIUS = 3


def extended(value, sides, width):
    for axis, dim in sides:
        peers, length = (lax.axis_size(axis), value.shape[dim])
        up = [(i, (i + 1) % peers) for i in range(peers - 1)]
        down = [(j, i) for i, j in up]
        last = lax.slice_in_dim(value, length - width, length, axis=dim)
        first = lax.slice_in_dim(value, 0, width, axis=dim)
        before = lax.ppermute(last, axis, up)
        after = lax.ppermute(first, axis, down)
        value = jnp.concatenate([before, value, after], axis=dim)
    return value


def gauss_taps():
    weights_raw = [math.exp(-0.5 * j * j) for j in range(-RADIUS, RADIUS + 1)]
    summed = sum(weights_raw)
    return [value / summed for value in weights_raw]


def taps_sum(padded, axis, length):
    coeffs = gauss_taps()
    running = coeffs[0] * lax.slice_in_dim(padded, 0, length, axis=axis)
    for offset_tap in range(1, 2 * RADIUS + 1):
        running = running + coeffs[offset_tap] * lax.slice_in_dim(
            padded, offset_tap, offset_tap + length, axis=axis
        )
    return running


def smooth_lateral(values):
    padded = jnp.pad(values, ((0, 0), (0, 0), (RADIUS, RADIUS), (0, 0)))
    values = taps_sum(padded, 2, values.shape[2])
    padded = jnp.pad(values, ((0, 0), (0, 0), (0, 0), (RADIUS, RADIUS)))
    return taps_sum(padded, 3, values.shape[3])


def laplace_rimmed(rimmed):
    center = rimmed[:, 1:-1]
    lateral = jnp.pad(center, ((0, 0), (0, 0), (1, 1), (1, 1)))
    beside = rimmed[:, 2:] + rimmed[:, :-2]
    beside = beside + lateral[:, :, 2:, 1:-1] + lateral[:, :, :-2, 1:-1]
    beside = beside + lateral[:, :, 1:-1, 2:] + lateral[:, :, 1:-1, :-2]
    return beside - 6.0 * center


def patchify(cube_block):
    chans, planes, height, across = cube_block.shape
    shaped = cube_block.reshape(chans, planes // 4, 4, height // 8, 8, across // 8, 8)
    shaped = shaped.transpose(1, 3, 5, 0, 2, 4, 6)
    return shaped.reshape(planes // 4 * (height // 8) * (across // 8), chans * 256)


def classify(hidden, expands, shrinks, heads):
    mix_up = "npk,kh->nph"
    mix_down = "nph,hk->npk"
    mix_head = "nk,kc->nc"
    wide = hidden.astype(jnp.float32)
    normed = (wide * lax.rsqrt(jnp.mean(wide * wide, axis=-1, keepdims=True) + 1e-05)).astype(
        jnp.bfloat16
    )
    up_part = expands[0]
    down_part = shrinks[0]
    expanded = jax.nn.relu(
        jnp.einsum(mix_up, normed, up_part, preferred_element_type=jnp.float32)
    ).astype(jnp.bfloat16)
    hidden = (
        wide + jnp.einsum(mix_down, expanded, down_part, preferred_element_type=jnp.float32)
    ).astype(jnp.bfloat16)
    pooled = jnp.mean(hidden.astype(jnp.float32), axis=1)
    return jnp.einsum(mix_head, pooled, heads.astype(jnp.float32), precision=lax.Precision.HIGHEST)


def body(
    volume,
    partner,
    offsets,
    starts,
    classifier,
    stem_weight,
    expand_weight,
    shrink_weight,
    head_weight,
):
    tile_count = lax.axis_size("tile")
    tile_me = lax.axis_index("tile")
    planes_dev, rows_dev, width_dev = (volume.shape[1], volume.shape[2], volume.shape[3])
    partner_tile = partner[tile_me]
    piece = lax.all_gather(volume[:, :, :, :OV], "tile", axis=0, tiled=True)
    tile_ids = jnp.arange(piece.shape[0], dtype=jnp.int32)
    selected = (tile_ids == partner_tile).astype(jnp.float32)[:, None, None, None]
    mate_strip = jnp.sum(piece.astype(jnp.float32) * selected, axis=0, keepdims=True)
    rows_back = (jnp.arange(rows_dev, dtype=jnp.int32) - offsets[tile_me]) % rows_dev
    mate_strip = jnp.take(mate_strip, rows_back, axis=2)
    values = volume.astype(jnp.float32)
    column = jnp.arange(OV, dtype=jnp.float32)
    ramp = 0.25 + 0.5 * (column + 0.5) / OV
    joined = jnp.concatenate(
        [ramp * values[..., :OV] + (1.0 - ramp) * mate_strip, values[..., OV:]], axis=3
    )
    rimmed = extended(joined.astype(jnp.bfloat16), (("slab", 1),), RADIUS).astype(joined.dtype)
    smooth = smooth_lateral(taps_sum(rimmed, 1, planes_dev))
    smooth_rimmed = extended(smooth, (("slab", 1),), 1)
    log_response = laplace_rimmed(smooth_rimmed)
    channel_pair = jnp.stack(
        [smooth[0].astype(jnp.bfloat16), log_response[0].astype(jnp.bfloat16)], axis=0
    )
    zero = jnp.zeros((), jnp.int32)

    def cut(begin):
        return patchify(
            lax.dynamic_slice(
                channel_pair, (zero, zero, zero, begin), (2, planes_dev, rows_dev, CX)
            )
        )

    routes = classifier[:, 0]
    cand_count = routes.shape[0]
    cand_ids = jnp.arange(cand_count, dtype=jnp.int32)
    same_dest = routes[:, None] == routes[None, :]
    earlier = cand_ids[None, :] < cand_ids[:, None]
    slot_rank = jnp.sum((same_dest & earlier).astype(jnp.int32), axis=1)
    slot_ids = routes * CAP + slot_rank
    slot_count = tile_count * CAP
    slot_hits = slot_ids[None, :] == jnp.arange(slot_count, dtype=jnp.int32)[:, None]
    filled = jnp.any(slot_hits, axis=1)
    source = jnp.sum(slot_hits.astype(jnp.int32) * cand_ids[None, :], axis=1)
    slot_patches = jax.vmap(cut)(starts[source]) * filled.astype(jnp.bfloat16)[:, None, None]
    slot_patches = slot_patches.reshape(
        tile_count, CAP, slot_patches.shape[1], slot_patches.shape[2]
    )
    pos_count = slot_patches.shape[2]
    arrived = lax.all_to_all(slot_patches, "tile", split_axis=0, concat_axis=0, tiled=True)
    senders = arrived.shape[0]
    items = arrived.shape[1]
    flat = arrived.reshape(senders * items, pos_count, arrived.shape[3])
    hidden = jnp.einsum(
        "npf,fk->npk", flat, stem_weight[0], preferred_element_type=jnp.float32
    ).astype(jnp.bfloat16)
    scores = classify(hidden, expand_weight[0], shrink_weight[0], head_weight[0])
    scored = scores.reshape(senders, items, scores.shape[1])
    returned = lax.all_to_all(scored, "tile", split_axis=0, concat_axis=0, tiled=True)
    logits = returned.reshape(slot_count, returned.shape[2])[slot_ids]
    return (log_response, logits)


def solution(mesh):
    return jax.shard_map(
        body,
        mesh=mesh,
        in_specs=(
            P("tile", "slab", None, None),
            P(),
            P(),
            P(("tile", "slab")),
            P(("tile", "slab"), None),
            P("tile", None, None),
            P("tile", None, None, None),
            P("tile", None, None, None),
            P("tile", None, None),
        ),
        out_specs=(P("tile", "slab", None, None), P(("tile", "slab"), None)),
        check_vma=False,
    )
```

profile of v0, /device:TPU:0, one launch (start us, length us, event | category | flops | bytes accessed | tf_op | source)
XLA Modules:
  0.0 439.4 jit_solution(5452797178134298504)
XLA Ops:
  0.7 1.4 copy_convert_fusion
  2.1 1.0 slice.101
  3.1 1.2 dynamic_slice.6
  4.3 0.7 fusion.60
  5.0 0.7 compare_and_fusion
  5.6 0.2 slice.292
  5.9 0.1 copy.50
  6.0 34.6 %all_gather.3 = bf16[8,16,64,32]{2,3,1,0:T(8,128)(2,1)S(1)} all-gather(bf16[1,16,64,32]{2,3,1,0:T(8,128)(2,1)S(1)} %copy.50), channel_id=1, replica_groups=mesh['tile'=8,'slab'=4] {'tile'}, dimensions={0}, use_global_device_ids=true | all-gather | bytes 589824 | tf_op jit(solution)/shard_map/all_gather | solution.py:103
  40.6 0.6 dynamic_slice.7
  41.2 0.6 compare_convert_fusion
  41.8 0.4 multiply_reduce_fusion
  42.2 0.3 copy.41
  42.5 0.6 gather_fusion
  43.1 0.2 fusion.47
  43.3 0.3 pad_maximum_fusion.4
  43.6 1.3 collective-permute-start.1
  44.9 3.0 collective-permute-start
  48.0 0.2 slice_bitcast_fusion
  48.2 0.2 convert_reduce_fusion.1
  48.4 0.1 select_reduce_fusion
  48.5 0.7 gather_fusion.1
  49.2 0.3 maximum_bitcast_fusion
  49.6 0.4 maximum_convert_fusion.1
  49.9 0.8 fusion.40
  50.8 0.3 fusion.16
  51.1 1.7 fusion.67
  52.9 3.4 collective-permute-start.3
  56.3 1.5 collective-permute-start.2
  58.0 3.4 collective-permute-done.2
  61.4 1.6 fusion.69
  63.0 1.1 pad_maximum_fusion.2
  64.0 4.6 %copy.42 = bf16[2,16,64,256]{2,1,0,3:T(8,128)(2,1)S(1)} copy(bf16[2,16,64,256]{3,1,2,0:T(8,128)(2,1)} %pad_maximum_fusion.2) | data formatting | bytes 2097152 | tf_op jit(solution)/shard_map/stack | solution.py:119
  68.6 4.9 %gather_fusion.2 = bf16[16,2,16,64,64]{3,2,1,4,0:T(8,128)(2,1)} fusion(bf16[2,16,64,256]{2,1,0,3:T(8,128)(2,1)S(1)} %copy.42, s32[16]{0:T(128)S(1)} %fusion.64), kind=kCustom, calls=%fused_computation.2 | custom fusion | bytes 8388864 | tf_op jit(solution)/shard_map/vmap()/gather | solution.py:126
  73.5 33.3 %copy.43 = bf16[16,2,16,64,64]{0,4,3,2,1:T(8,128)(2,1)} copy(bf16[16,2,16,64,64]{3,2,1,4,0:T(8,128)(2,1)} %gather_fusion.2) | data formatting | bytes 8388608 | tf_op jit(solution)/shard_map/vmap()/gather | solution.py:126
  106.8 108.3 %copy.44 = bf16[16,4,8,8,2,4,8,8]{7,6,5,4,3,2,1,0:T(8,128)(2,1)} copy(bf16[16,4,8,8,2,4,8,8]{0,7,3,6,2,5,1,4:T(8,128)(2,1)} %bitcast.62) | data formatting | bytes 8388608 | tf_op jit(solution)/shard_map/vmap()/transpose | solution.py:64
  215.1 95.3 %reshape.257 = bf16[8,2,256,512]{3,2,1,0:T(8,128)(2,1)} reshape(bf16[16,4,8,8,2,4,8,8]{7,6,5,4,3,2,1,0:T(8,128)(2,1)} %copy.44) | data formatting | bytes 8388608 | tf_op jit(solution)/shard_map/vmap()/reshape | solution.py:65
  310.4 4.5 %broadcast_multiply_fusion = bf16[8,2,256,512]{3,2,1,0:T(8,128)(2,1)} fusion(bf16[8,2,256,512]{3,2,1,0:T(8,128)(2,1)} %reshape.257, bf16[8,2]{1,0:T(8,128)(2,1)S(1)} %reshape.260), kind=kLoop, calls=%fused_computation.24 | loop fusion | flops 2097152 | bytes 8388640 | tf_op jit(solution)/shard_map/mul | solution.py:142
  314.9 5.6 %all-to-all-start = ((bf16[8,2,256,512]{3,2,1,0:T(8,128)(2,1)}), bf16[8,2,256,512]{3,2,1,0:T(8,128)(2,1)}, u32[]{:S(2)}, u32[]{:S(2)}) async-start(bf16[8,2,256,512]{3,2,1,0:T(8,128)(2,1)} %broadcast_multiply_fusion), calls=%async_computation | async-start | bytes 8388608 | tf_op jit(solution)/shard_map/all_to_all | solution.py:147
  320.5 93.4 %all-to-all-done = bf16[8,2,256,512]{3,2,1,0:T(8,128)(2,1)} async-done(((bf16[8,2,256,512]{3,2,1,0:T(8,128)(2,1)}), bf16[8,2,256,512]{3,2,1,0:T(8,128)(2,1)}, u32[]{:S(2)}, u32[]{:S(2)}) %all-to-all-start) | async-done | bytes 4194336 | tf_op jit(solution)/shard_map/all_to_all | solution.py:147
  413.9 4.8 %fusion = (f32[16,256]{1,0:T(8,128)S(1)}, bf16[16,256,256]{2,1,0:T(8,128)(2,1)}) fusion(bf16[16,256,512]{2,1,0:T(8,128)(2,1)} %bitcast.15, bf16[1,512,256]{2,1,0:T(8,128)(2,1)S(1)} %copy-done.5), kind=kOutput, calls=%fused_computation.8 | convolution fusion | flops 1077932032 | bytes 6569984 | tf_op jit(solution)/shard_map/npf,fk->npk/dot_general | solution.py:151
  418.8 7.2 %convert_reduce_fusion = f32[16,256]{1,0:T(8,128)S(1)} fusion(bf16[16,256,256]{2,1,0:T(8,128)(2,1)} %get-tuple-element.19, f32[16,256]{1,0:T(8,128)S(1)} %add_rsqrt_fusion, bf16[1,1,1024,256]{3,2,1,0:T(8,128)(2,1)S(1)} %copy-done, bf16[1,1,256,1024]{3,2,1,0:T(8,128)(2,1)S(1)} %copy-done.4), kind=kOutput, calls=%fused_computation.11 | convolution fusion | flops 4311740416 | bytes 3178496 | tf_op jit(solution)/shard_map/nph,hk->npk/dot_general | solution.py:82
  426.1 0.1 fusion.53
  426.2 0.6 copy.46
  426.8 4.8 %all-to-all-start.1 = ((f32[8,2,8]{2,1,0:T(2,128)}), f32[8,2,8]{2,1,0:T(2,128)S(1)}, u32[]{:S(2)}, u32[]{:S(2)}) async-start(f32[8,2,8]{2,1,0:T(2,128)} %copy.46), calls=%async_computation.1 | async-start | bytes 16384 | tf_op jit(solution)/shard_map/all_to_all | solution.py:156
  431.7 1.6 copy.47
  433.3 4.9 %all-to-all-done.1 = f32[8,2,8]{2,1,0:T(2,128)S(1)} async-done(((f32[8,2,8]{2,1,0:T(2,128)}), f32[8,2,8]{2,1,0:T(2,128)S(1)}, u32[]{:S(2)}, u32[]{:S(2)}) %all-to-all-start.1) | async-done | bytes 544 | tf_op jit(solution)/shard_map/all_to_all | solution.py:156
  438.2 0.6 gather_fusion.3
  438.7 0.7 copy.48
  (34 shorter events, 0.4 us)
Async XLA Ops:
  0.6 418.2 %copy-start = (bf16[1,1,1024,256]{3,2,1,0:T(8,128)(2,1)S(1)}, bf16[1,1,1024,256]{3,2,1,0:T(8,128)(2,1)}, u32[]{:S(2)}) copy-start(bf16[1,1,1024,256]{3,2,1,0:T(8,128)(2,1)} %param.16) | copy-start | bytes 1572868
  0.6 40.0 %copy-start.6 = (s32[8]{0:T(128)S(1)}, s32[8]{0:T(128)}, u32[]{:S(2)}) copy-start(s32[8]{0:T(128)} %param.10) | copy-start | bytes 100
  5.9 42.3 %copy-start.7 = (s32[16,1]{0,1:T(1,128)S(1)}, s32[16,1]{0,1:T(1,128)}, u32[]{:S(2)}) copy-start(s32[16,1]{0,1:T(1,128)} %param.13) | copy-start | bytes 196
  5.9 42.7 %copy-start.1 = (s32[16]{0:T(128)S(1)}, s32[16]{0:T(128)}, u32[]{:S(2)}) copy-start(s32[16]{0:T(128)} %param.12) | copy-start | bytes 196
  43.6 5.9 %collective-permute-start.1 = (bf16[1,3,64,256]{3,1,2,0:T(4,128)(2,1)S(1)}, bf16[1,3,64,256]{3,1,2,0:T(4,128)(2,1)S(1)}, u32[]{:S(2)}, u32[]{:S(2)}) collective-permute-start(bf16[1,3,64,256]{3,1,2,0:T(4,128)(2,1)S(1)} %get-tuple-element.17), channel_id=1, source_target_pairs={{1,0},{2,1},{3,2},{5,4},{6,5},{7,6},{9,8},{10,9},{11,10},{13,12},{... | collective-permute-start | bytes 294920 | tf_op jit(solution)/shard_map/ppermute | solution.py:24
  44.9 4.6 %collective-permute-start = (bf16[1,3,64,256]{3,1,2,0:T(4,128)(2,1)S(1)}, bf16[1,3,64,256]{3,1,2,0:T(4,128)(2,1)S(1)}, u32[]{:S(2)}, u32[]{:S(2)}) collective-permute-start(bf16[1,3,64,256]{3,1,2,0:T(4,128)(2,1)S(1)} %get-tuple-element.16), channel_id=1, source_target_pairs={{0,1},{1,2},{2,3},{4,5},{5,6},{6,7},{8,9},{9,10},{10,11},{12,13},{... | collective-permute-start | bytes 294920 | tf_op jit(solution)/shard_map/ppermute | solution.py:23
  52.9 5.1 %collective-permute-start.3 = (f32[1,1,64,256]{3,1,2,0:T(1,128)S(1)}, f32[1,1,64,256]{3,1,2,0:T(1,128)S(1)}, u32[]{:S(2)}, u32[]{:S(2)}) collective-permute-start(f32[1,1,64,256]{3,1,2,0:T(1,128)S(1)} %get-tuple-element.15), channel_id=1, source_target_pairs={{0,1},{1,2},{2,3},{4,5},{5,6},{6,7},{8,9},{9,10},{10,11},{12,13},{... | collective-permute-start | bytes 196616 | tf_op jit(solution)/shard_map/ppermute | solution.py:23
  56.3 5.1 %collective-permute-start.2 = (f32[1,1,64,256]{3,1,2,0:T(1,128)S(1)}, f32[1,1,64,256]{3,1,2,0:T(1,128)S(1)}, u32[]{:S(2)}, u32[]{:S(2)}) collective-permute-start(f32[1,1,64,256]{3,1,2,0:T(1,128)S(1)} %get-tuple-element.14), channel_id=1, source_target_pairs={{1,0},{2,1},{3,2},{5,4},{6,5},{7,6},{9,8},{10,9},{11,10},{13,12},{... | collective-permute-start | bytes 196616 | tf_op jit(solution)/shard_map/ppermute | solution.py:24
  314.9 99.0 %copy-start.5 = (bf16[1,512,256]{2,1,0:T(8,128)(2,1)S(1)}, bf16[1,512,256]{2,1,0:T(8,128)(2,1)}, u32[]{:S(2)}) copy-start(bf16[1,512,256]{2,1,0:T(8,128)(2,1)} %param.14) | copy-start | bytes 786436
  314.9 99.0 %all-to-all-start = ((bf16[8,2,256,512]{3,2,1,0:T(8,128)(2,1)}), bf16[8,2,256,512]{3,2,1,0:T(8,128)(2,1)}, u32[]{:S(2)}, u32[]{:S(2)}) async-start(bf16[8,2,256,512]{3,2,1,0:T(8,128)(2,1)} %broadcast_multiply_fusion), calls=%async_computation | async-start | bytes 8388608 | tf_op jit(solution)/shard_map/all_to_all | solution.py:147
  413.9 4.9 %copy-start.4 = (bf16[1,1,256,1024]{3,2,1,0:T(8,128)(2,1)S(1)}, bf16[1,1,256,1024]{3,2,1,0:T(8,128)(2,1)}, u32[]{:S(2)}) copy-start(bf16[1,1,256,1024]{3,2,1,0:T(8,128)(2,1)} %param.15) | copy-start | bytes 1572868
  418.8 7.3 %copy-start.3 = (bf16[1,256,8]{1,2,0:T(8,128)(2,1)S(1)}, bf16[1,256,8]{1,2,0:T(8,128)(2,1)}, u32[]{:S(2)}) copy-start(bf16[1,256,8]{1,2,0:T(8,128)(2,1)} %param.17) | copy-start | bytes 12292
  418.8 12.9 %copy-start.2 = (f32[1,16,64,256]{3,1,2,0:T(8,128)S(1)}, f32[1,16,64,256]{3,1,2,0:T(8,128)}, u32[]{:S(2)}) copy-start(f32[1,16,64,256]{3,1,2,0:T(8,128)} %get-tuple-element.13) | copy-start | bytes 3145732
  426.8 11.3 %all-to-all-start.1 = ((f32[8,2,8]{2,1,0:T(2,128)}), f32[8,2,8]{2,1,0:T(2,128)S(1)}, u32[]{:S(2)}, u32[]{:S(2)}) async-start(f32[8,2,8]{2,1,0:T(2,128)} %copy.46), calls=%async_computation.1 | async-start | bytes 16384 | tf_op jit(solution)/shard_map/all_to_all | solution.py:156
where the time goes:
time: 441 us; the launch traced here: 439 us
  local copies, waits for them, and re-layouts  255 us (58%)
  waiting for transfers between devices  102 us (23%)
  blocking collectives  34.6 us (8%)
  starting transfers between devices  19.6 us (4%)
  other arithmetic  15.4 us (3%)
  matrix products  12.2 us (3%)
    transpose x1, local copies, waits for them, and re-layouts, patchify(): shaped = shaped.transpose(1, 3, 5, 0, 2, 4, 6)  108 us
    reshape x1, local copies, waits for them, and re-layouts, patchify(): shaped.reshape(planes // 4 * (height // 8) * (across // 8), chans * 256)  95.3 us
    all_to_all x1, waiting for transfers between devices, body(): lax.all_to_all(slot_patches, 'tile', split_axis=0, concat_axis=0, tiled=T...  93.4 us
    gather x2, local copies, waits for them, and re-layouts, cut(): lax.dynamic_slice(channel_pair, (zero, zero, zero, begin), (2, planes_dev...  38.2 us
    all_gather x1, blocking collectives, body(): piece = lax.all_gather(volume[:, :, :, :OV], 'tile', axis=0, tiled=True)  34.6 us
  transfers between devices with their start and end apart: 6, of which 3 were waited for; matrix products, arithmetic and copies ran while one was open for 1% of the time, Pallas kernels for 0%

commit v1 on v0

v1 whole, which is shorter than its diff:
```python
import functools
import math

import jax
import jax.numpy as jnp
from jax import lax
from jax.experimental import pallas as pl
from jax.experimental.pallas import tpu as pltpu
from jax.sharding import PartitionSpec as P

OV = 32
RADIUS = 3
HALO = RADIUS + 1
PAD = 8


def gauss_taps():
    weights_raw = [math.exp(-0.5 * j * j) for j in range(-RADIUS, RADIUS + 1)]
    summed = sum(weights_raw)
    return [value / summed for value in weights_raw]


def band_kernel(flags_ref, joined_ref, band_ref, log_ref, table_ref, smooth, lateral, turned):
    planes, rows, width = log_ref.shape
    taps = gauss_taps()
    zero_rows = jnp.zeros((PAD, width), jnp.float32)

    lateral[0:PAD] = zero_rows
    lateral[PAD + rows :] = zero_rows

    @pl.loop(0, planes + 2)
    def _(z):
        total = taps[RADIUS] * joined_ref[z + RADIUS]
        for j in range(RADIUS):
            total = total + taps[j] * (joined_ref[z + j] + joined_ref[z + 2 * RADIUS - j])
        lateral[PAD : PAD + rows] = total
        down = taps[RADIUS] * total
        for j in range(RADIUS):
            shift = RADIUS - j
            down = down + taps[j] * (
                lateral[PAD - shift : PAD - shift + rows] + lateral[PAD + shift : PAD + shift + rows]
            )
        across = jnp.dot(
            down, band_ref[...], precision=lax.Precision.HIGHEST, preferred_element_type=jnp.float32
        )
        keep = jnp.where(z == 0, flags_ref[0], jnp.where(z == planes + 1, flags_ref[1], 1.0))
        smooth[z, 0:PAD] = zero_rows
        smooth[z, PAD + rows :] = zero_rows
        smooth[z, PAD : PAD + rows] = across * keep

    column = lax.broadcasted_iota(jnp.int32, (rows, width), 1)

    @pl.loop(0, planes)
    def _(z):
        center = smooth[z + 1, PAD : PAD + rows]
        beside = smooth[z, PAD : PAD + rows] + smooth[z + 2, PAD : PAD + rows]
        beside = beside + smooth[z + 1, PAD + 1 : PAD + 1 + rows] + smooth[z + 1, PAD - 1 : PAD - 1 + rows]
        right = jnp.where(column == width - 1, 0.0, pltpu.roll(center, width - 1, 1))
        left = jnp.where(column == 0, 0.0, pltpu.roll(center, 1, 1))
        log_ref[z] = beside + right + left - 6.0 * center

    pitch = turned.shape[0] // (planes // 4 * (rows // 8))

    @pl.loop(0, planes // 4)
    def _(a):
        for b in range(rows // 8):
            parts = [smooth[4 * a + dz + 1, PAD + 8 * b : PAD + 8 * b + 8] for dz in range(4)]
            parts = parts + [log_ref[4 * a + dz, 8 * b : 8 * b + 8] for dz in range(4)]
            block = jnp.concatenate(parts, axis=0)
            block = jnp.concatenate([block, pltpu.roll(block, width - 1, 1)], axis=0)
            start = pl.multiple_of((a * (rows // 8) + b) * pitch, 8)
            turned[pl.ds(start, width)] = block.T

    spots = planes // 4 * (rows // 8)

    @pl.loop(0, width // 8)
    def _(xb):
        for u in range(8):
            x = xb * 8 + u
            table_ref[x] = turned[pl.ds(x, spots, stride=pitch), :].astype(jnp.bfloat16)


def classify_kernel(starts_ref, routes_ref, table_ref, weights_ref, out_ref):
    slabs = weights_ref.shape[1]
    stem_rows, expand_rows, shrink_rows = 512 // slabs, 256 // slabs, 1024 // slabs

    def rows_of(route, first, length):
        return jnp.concatenate([weights_ref[route, s, first : first + length] for s in range(slabs)], axis=0)

    @pl.loop(0, out_ref.shape[0])
    def _(i):
        start = starts_ref[i]
        route = routes_ref[i]
        patches = jnp.concatenate(
            [
                jnp.concatenate([table_ref[start + 8 * c + 2 * j] for j in range(4)], axis=1)
                for c in range(8)
            ],
            axis=0,
        )
        stem = rows_of(route, 0, stem_rows)
        hidden = jnp.dot(patches, stem, preferred_element_type=jnp.float32).astype(jnp.bfloat16)
        wide = hidden.astype(jnp.float32)
        scale = lax.rsqrt(jnp.mean(wide * wide, axis=1, keepdims=True) + 1e-05)
        normed = (wide * scale).astype(jnp.bfloat16)
        expanded = []
        for block in range(4):
            expand = rows_of(route, stem_rows + block * expand_rows, expand_rows)
            wider = jnp.dot(normed, expand, preferred_element_type=jnp.float32)
            expanded.append(jnp.maximum(wider, 0.0).astype(jnp.bfloat16))
        shrink = rows_of(route, stem_rows + 4 * expand_rows, shrink_rows)
        added = jnp.dot(jnp.concatenate(expanded, axis=1), shrink, preferred_element_type=jnp.float32)
        last = (wide + added).astype(jnp.bfloat16).astype(jnp.float32)
        head = weights_ref[route, 0, stem_rows + 4 * expand_rows + shrink_rows :].astype(jnp.float32)
        total = head[0:8] * jnp.sum(last, axis=0, keepdims=True)
        score = jnp.sum(total, axis=1, keepdims=True) * (1.0 / patches.shape[0])
        out_ref[i] = jnp.broadcast_to(score, out_ref.shape[1:])


def own_weights(stem_weight, expand_weight, shrink_weight, head_weight):
    slabs, slab_me = lax.axis_size("slab"), lax.axis_index("slab")
    stem, expand, shrink, head = stem_weight[0], expand_weight[0, 0], shrink_weight[0, 0], head_weight[0]
    stem = lax.dynamic_slice_in_dim(stem.reshape(64, 8, 256), slab_me * (8 // slabs), 8 // slabs, axis=1)
    stem = stem.transpose(1, 0, 2).reshape(512 // slabs, 256)
    expand = lax.dynamic_slice_in_dim(expand, slab_me * (256 // slabs), 256 // slabs, axis=0)
    expand = [expand[:, 256 * m : 256 * m + 256] for m in range(4)]
    shrink = lax.dynamic_slice_in_dim(shrink, slab_me * (1024 // slabs), 1024 // slabs, axis=0)
    head = jnp.pad(head.T, ((0, 8), (0, 0)))
    return jnp.concatenate([stem] + expand + [shrink, head], axis=0)


def body(
    volume,
    partner,
    offsets,
    starts,
    classifier,
    stem_weight,
    expand_weight,
    shrink_weight,
    head_weight,
):
    slabs, slab_me = lax.axis_size("slab"), lax.axis_index("slab")
    tiles, tile_me = lax.axis_size("tile"), lax.axis_index("tile")
    planes, rows, width = volume.shape[1:]
    raw = volume[0]

    up = [(i, i + 1) for i in range(slabs - 1)]
    down = [(i + 1, i) for i in range(slabs - 1)]
    before = lax.ppermute(raw[planes - HALO :], "slab", up)
    after = lax.ppermute(raw[:HALO], "slab", down)
    raw = jnp.concatenate([before, raw, after], axis=0)
    deep = planes + 2 * HALO
    strips = lax.all_gather(raw[:, :, :OV], "tile", axis=0)

    share = own_weights(stem_weight, expand_weight, shrink_weight, head_weight)
    weights = lax.all_gather(share, ("tile", "slab"), axis=0)
    weights = weights.reshape(tiles, slabs, share.shape[0], 256)

    mate = lax.dynamic_index_in_dim(strips, partner[tile_me], 0, keepdims=False)
    mate = lax.dynamic_slice_in_dim(
        jnp.concatenate([mate, mate], axis=1), rows - offsets[tile_me], rows, axis=1
    ).astype(jnp.float32)
    ramp = 0.25 + 0.5 * (jnp.arange(OV, dtype=jnp.float32) + 0.5) / OV
    values = raw.astype(jnp.float32)
    joined = jnp.concatenate(
        [ramp * values[..., :OV] + (1.0 - ramp) * mate, values[..., OV:]], axis=2
    )

    taps = gauss_taps()
    apart = jnp.arange(width)[:, None] - jnp.arange(width)[None, :]
    band = sum(jnp.where(apart == j - RADIUS, taps[j], 0.0) for j in range(2 * RADIUS + 1))
    flags = jnp.stack([slab_me > 0, slab_me < slabs - 1]).astype(jnp.float32)
    spots = planes // 4 * (rows // 8)
    vmem = pl.BlockSpec(memory_space=pltpu.VMEM)
    smem = pl.BlockSpec(memory_space=pltpu.SMEM)
    log_response, table = pl.pallas_call(
        band_kernel,
        out_shape=(
            jax.ShapeDtypeStruct((planes, rows, width), jnp.float32),
            jax.ShapeDtypeStruct((width, spots, 128), jnp.bfloat16),
        ),
        in_specs=[smem, vmem, vmem],
        out_specs=(vmem, vmem),
        scratch_shapes=[
            pltpu.VMEM((planes + 2, rows + 2 * PAD, width), jnp.float32),
            pltpu.VMEM((rows + 2 * PAD, width), jnp.float32),
            pltpu.VMEM((spots * (width + 8), 128), jnp.float32),
        ],
        compiler_params=pltpu.CompilerParams(vmem_limit_bytes=48 * 1024 * 1024),
        cost_estimate=pl.CostEstimate(flops=10**9, bytes_accessed=6 * 10**6, transcendentals=0),
        name="band",
    )(flags, joined, band)

    count = starts.shape[0]
    scores = pl.pallas_call(
        classify_kernel,
        out_shape=jax.ShapeDtypeStruct((count, 8, 128), jnp.float32),
        in_specs=[smem, smem, vmem, vmem],
        out_specs=vmem,
        compiler_params=pltpu.CompilerParams(vmem_limit_bytes=48 * 1024 * 1024),
        cost_estimate=pl.CostEstimate(flops=54 * 10**8, bytes_accessed=13 * 10**6, transcendentals=0),
        name="classify",
    )(starts, classifier[:, 0], table, weights)
    return log_response[None], scores[:, :, 0]


def solution(mesh):
    return jax.shard_map(
        body,
        mesh=mesh,
        in_specs=(
            P("tile", "slab", None, None),
            P(),
            P(),
            P(("tile", "slab")),
            P(("tile", "slab"), None),
            P("tile", None, None),
            P("tile", None, None, None),
            P("tile", None, None, None),
            P("tile", None, None),
        ),
        out_specs=(P("tile", "slab", None, None), P(("tile", "slab"), None)),
        check_vma=False,
    )
```

time: 441 us -> 139 us (0.32)
  local copies, waits for them, and re-layouts: 255 us -> 8.88 us
  waiting for transfers between devices: 102 us -> 29.4 us
  Pallas kernels: 0 us -> 31.2 us
  between operations: 0.95 us -> 17.4 us
  starting transfers between devices: 19.6 us -> 4.37 us
  other arithmetic: 15.4 us -> 1.19 us
  matrix products: 12.2 us -> 0 us
  blocking collectives: 34.6 us -> 45.7 us
    transpose x1 -> x2, local copies, waits for them, and re-layouts: 108 us -> 1.11 us  [own_weights(): stem = stem.transpose(1, 0, 2).reshape(512 // slabs, 256)]
    all_to_all x2 -> x0, waiting for transfers between devices: 98.3 us -> none  [the longest x1 93.4 us: body(): lax.all_to_all(slot_patches, 'tile', split_axis=0, concat_axis=0, tiled=T...]
    reshape x1 -> x0, local copies, waits for them, and re-layouts: 95.3 us -> none  [patchify(): shaped.reshape(planes // 4 * (height // 8) * (across // 8), chans * 256)]
    gather x5 -> x0, local copies, waits for them, and re-layouts: 40.1 us -> none  [the longest x2 38.2 us: cut(): lax.dynamic_slice(channel_pair, (zero, zero, zero, begin), (2, planes_dev...]
    pallas_call x0 -> x2, Pallas kernels: none -> 31.2 us  [the longest x1 19 us: body(): pl.pallas_call(classify_kernel, out_shape=jax.ShapeDtypeStruct((count, 8,...]
    all_gather x0 -> x1, waiting for transfers between devices: none -> 29.4 us  [body(): weights = lax.all_gather(share, ('tile', 'slab'), axis=0)]
    dot_general x3 -> x0, matrix products: 12.2 us -> none  [the longest x1 7.21 us: classify(): jnp.einsum(mix_down, expanded, down_part, preferred_element_type=jnp.floa...]
    all_gather x1, blocking collectives: 34.6 us -> 45.7 us  [body(): strips = lax.all_gather(raw[:, :, :OV], 'tile', axis=0)]
  transfers between devices with their start and end apart: 6 -> 3, of which waited for: 3 -> 1; matrix products, arithmetic and copies ran while one was open for 1% -> 3% of each run, Pallas kernels for 0% -> 9%
where the time goes in v1:
time: 139 us; the launch traced here: 138 us
  blocking collectives  45.7 us (33%)
  Pallas kernels  31.2 us (22%)
  waiting for transfers between devices  29.4 us (21%)
  between operations  17.4 us (13%)
  local copies, waits for them, and re-layouts  8.88 us (6%)
  starting transfers between devices  4.37 us (3%)
    all_gather x1, blocking collectives, body(): strips = lax.all_gather(raw[:, :, :OV], 'tile', axis=0)  45.7 us
    all_gather x1, waiting for transfers between devices, body(): weights = lax.all_gather(share, ('tile', 'slab'), axis=0)  29.4 us
    pallas_call x1, Pallas kernels, body(): pl.pallas_call(classify_kernel, out_shape=jax.ShapeDtypeStruct((count, 8,...  19 us
    pallas_call x1, Pallas kernels, body(): pl.pallas_call(band_kernel, out_shape=(jax.ShapeDtypeStruct((planes, rows...  12.2 us
    unnamed x23, local copies, waits for them, and re-layouts  3.24 us
    ppermute x1, starting transfers between devices, body(): before = lax.ppermute(raw[planes - HALO:], 'slab', up)  3.04 us
  transfers between devices with their start and end apart: 3, of which 1 were waited for; matrix products, arithmetic and copies ran while one was open for 3% of the time, Pallas kernels for 9%

profile of v1, /device:TPU:0, one launch (start us, length us, event | category | flops | bytes accessed | tf_op | source)
XLA Modules:
  0.0 138.2 jit_solution(4778450575733294231)
XLA Ops:
  7.2 0.0 copy-start
  7.2 0.0 copy-start.4
  7.2 0.0 copy-start.6
  7.2 0.0 copy-start.7
  7.2 0.0 all-gather.4.cloned.1.call-start
  7.3 1.1 dynamic-slice_bitcast_fusion.2
  8.4 0.0 copy-done
  8.5 0.9 bitcast_dynamic-update-slice_fusion
  9.4 0.7 constant_dynamic-update-slice_fusion
  10.1 0.0 copy-start.5
  10.1 0.7 copy-done.5
  10.9 0.0 all-gather.4.cloned.1.call-update
  10.9 0.0 copy-done.4
  10.9 1.3 collective-permute-start.1
  12.2 3.0 %collective-permute-start = (bf16[4,64,256]{2,1,0:T(8,128)(2,1)S(1)}, bf16[4,64,256]{2,1,0:T(8,128)(2,1)S(1)}, u32[]{:S(2)}, u32[]{:S(2)}) collective-permute-start(bf16[4,64,256]{2,1,0:T(8,128)(2,1)S(1)} %get-tuple-element.8), channel_id=1, source_target_pairs={{0,1},{1,2},{2,3},{4,5},{5,6},{6,7},{8,9},{9,10},{10,11},{12,13},{... | collective-permute-start | bytes 393224 | tf_op jit(solution)/shard_map/ppermute | solution.py:150
  15.3 0.1 add_convert_fusion.flags_ref
  15.4 0.0 copy-done.6
  15.4 0.6 dynamic_slice.26
  17.2 0.0 copy-done.7
  17.2 0.6 dynamic_slice.28
  19.7 0.1 select_add_fusion.band_ref
  19.8 0.0 collective-permute-done.1
  19.8 0.0 collective-permute-done
  19.9 0.2 pad_maximum_fusion.1
  20.0 1.6 %slice.50 = f32[24,64,224]{2,1,0:T(8,128)} slice(f32[24,64,256]{2,1,0:T(8,128)S(1)} %get-tuple-element.7), slice={[0:24], [0:64], [32:256]} | slice | bytes 2752512 | tf_op jit(solution)/shard_map/slice | solution.py:167
  21.6 0.1 slice.49
  21.7 0.2 copy.13
  21.9 45.7 %all-gather = bf16[192,64,32]{1,2,0:T(8,128)(2,1)S(1)} all-gather(bf16[24,64,32]{1,2,0:T(8,128)(2,1)S(1)} %copy.13), channel_id=2, replica_groups=mesh['tile'=8,'slab'=4] {'tile'}, dimensions={0}, use_global_device_ids=true | all-gather | bytes 884736 | tf_op jit(solution)/shard_map/all_gather | solution.py:154
  67.6 0.2 dynamic-slice_maximum_fusion
  67.9 0.2 copy.17
  68.1 0.0 copy-start.3
  68.1 0.1 fusion
  68.3 1.3 copy-done.3
  69.5 0.5 pad_maximum_fusion.joined_ref
  70.0 0.0 copy-start.1
  70.0 0.0 copy-start.2
  70.0 12.2 %band.1 = (f32[16,64,256]{2,1,0:T(8,128)}, bf16[256,32,128]{2,1,0:T(8,128)(2,1)S(1)}) custom-call(f32[2]{0:T(128)S(1)} %add_convert_fusion.flags_ref, f32[24,64,256]{2,1,0:T(8,128)S(1)} %pad_maximum_fusion.joined_ref, f32[256,256]{1,0:T(8,128)S(1)} %select_add_fusion.band_ref), custom_call_target="tpu_custom_call" | custom-call | flops 1000000000 | bytes 6000000 | tf_op jit(solution)/shard_map/band/pallas_call | solution.py:177
  82.3 29.4 %all-gather.4.cloned.1.call-done = bf16[20992,256]{1,0:T(8,128)(2,1)} async-done(((bf16[656,256]{1,0:T(8,128)(2,1)}), bf16[20992,256]{1,0:T(8,128)(2,1)}) %all-gather.4.cloned.1.call-update) | async-done | bytes 10747920 | tf_op jit(solution)/shard_map/all_gather | solution.py:157
  111.6 0.0 copy-done.1
  111.6 0.0 copy-done.2
  111.6 19.0 %classify.1 = f32[16,8,128]{2,1,0:T(8,128)S(1)} custom-call(s32[16]{0:T(128)S(1)} %copy-done.1, s32[16]{0:T(128)S(1)} %bitcast.30, bf16[256,32,128]{2,1,0:T(8,128)(2,1)S(1)} %get-tuple-element.5.table_ref, bf16[8,4,656,256]{3,2,1,0:T(8,128)(2,1)} %bitcast.37), custom_call_target="tpu_custom_call" | custom-call | flops 5400000000 | bytes 13000000 | tf_op jit(solution)/shard_map/classify/pallas_call | solution.py:196
  130.7 0.7 copy.16
  (10 shorter events, 0.1 us)
Async XLA Ops:
  7.2 1.2 copy-start
  7.2 3.7 %copy-start.4 = (bf16[1,16,64,256]{3,2,1,0:T(8,128)(2,1)S(1)}, bf16[1,16,64,256]{3,2,1,0:T(8,128)(2,1)}, u32[]{:S(2)}) copy-start(bf16[1,16,64,256]{3,2,1,0:T(8,128)(2,1)} %param.9) | copy-start | bytes 1572868
  7.2 8.2 %copy-start.6 = (s32[8]{0:T(128)S(1)}, s32[8]{0:T(128)}, u32[]{:S(2)}) copy-start(s32[8]{0:T(128)} %param.10) | copy-start | bytes 100
  7.2 10.0 %copy-start.7 = (s32[8]{0:T(128)S(1)}, s32[8]{0:T(128)}, u32[]{:S(2)}) copy-start(s32[8]{0:T(128)} %param.11) | copy-start | bytes 100
  7.2 104.4 %all-gather.4.cloned.1.call-start = ((), (), s32[]{:S(2)}) async-start(), calls=%async_computation | async-start | bytes 11083776 | tf_op jit(solution)/shard_map/all_gather | solution.py:157
  10.1 0.7 copy-start.5
  10.9 8.9 %collective-permute-start.1 = (bf16[4,64,256]{2,1,0:T(8,128)(2,1)S(1)}, bf16[4,64,256]{2,1,0:T(8,128)(2,1)S(1)}, u32[]{:S(2)}, u32[]{:S(2)}) collective-permute-start(bf16[4,64,256]{2,1,0:T(8,128)(2,1)S(1)} %get-tuple-element.9), channel_id=1, source_target_pairs={{1,0},{2,1},{3,2},{5,4},{6,5},{7,6},{9,8},{10,9},{11,10},{13,12},{... | collective-permute-start | bytes 393224 | tf_op jit(solution)/shard_map/ppermute | solution.py:151
  12.2 7.6 %collective-permute-start = (bf16[4,64,256]{2,1,0:T(8,128)(2,1)S(1)}, bf16[4,64,256]{2,1,0:T(8,128)(2,1)S(1)}, u32[]{:S(2)}, u32[]{:S(2)}) collective-permute-start(bf16[4,64,256]{2,1,0:T(8,128)(2,1)S(1)} %get-tuple-element.8), channel_id=1, source_target_pairs={{0,1},{1,2},{2,3},{4,5},{5,6},{6,7},{8,9},{9,10},{10,11},{12,13},{... | collective-permute-start | bytes 393224 | tf_op jit(solution)/shard_map/ppermute | solution.py:150
  68.1 1.4 %copy-start.3 = (f32[24,64,224]{2,1,0:T(8,128)S(1)}, f32[24,64,224]{2,1,0:T(8,128)}, u32[]{:S(2)}) copy-start(f32[24,64,224]{2,1,0:T(8,128)} %slice.50) | copy-start | bytes 4128772
  70.0 41.6 %copy-start.1 = (s32[16]{0:T(128)S(1)}, s32[16]{0:T(128)}, u32[]{:S(2)}) copy-start(s32[16]{0:T(128)} %starts_ref.1) | copy-start | bytes 196
  70.0 41.6 %copy-start.2 = (s32[16,1]{0,1:T(1,128)S(1)}, s32[16,1]{0,1:T(1,128)}, u32[]{:S(2)}) copy-start(s32[16,1]{0,1:T(1,128)} %param.13) | copy-start | bytes 196
Sparse Core Ops, SparseCore 0:
  11.0 100.5 all-gather.3

commit v2 on v1

--- a/solution.py
+++ b/solution.py
@@ -80,12 +80,99 @@
             table_ref[x] = turned[pl.ds(x, spots, stride=pitch), :].astype(jnp.bfloat16)
 
 
+def gather_kernel(own_w, own_s, w_ref, s_ref, sems, local):
+    tile, slab = lax.axis_index("tile"), lax.axis_index("slab")
+    depth = lax.axis_size("tile") // 2
+    z, y, x, core = tile // 2, tile % 2, slab // 2, slab % 2
+    above, below = (tile + 2, slab), (tile - 2, slab)
+    beside, across, twin = (2 * z + 1 - y, slab), (tile, 2 * (1 - x) + core), (tile, 2 * x + 1 - core)
+    local_w = pltpu.make_async_copy(own_w, w_ref.at[tile], local.at[0])
+    local_s = pltpu.make_async_copy(own_s, s_ref.at[tile], local.at[1])
+    local_w.start()
+    local_s.start()
+    barrier = pltpu.get_barrier_semaphore()
+
+    def greet(peer):
+        pl.semaphore_signal(barrier, inc=1, device_id=peer, device_id_type=pl.DeviceIdType.MESH)
+
+    for peer in (beside, across, twin):
+        greet(peer)
+    pl.when(z < depth - 1)(lambda: greet(above))
+    pl.when(z > 0)(lambda: greet(below))
+    ends = jnp.where(z == 0, 1, 0) + jnp.where(z == depth - 1, 1, 0)
+    pl.semaphore_wait(barrier, 5 - ends)
+    local_s.wait()
+    local_w.wait()
+
+    def plane_part(origin):
+        return w_ref.at[origin, pl.ds(core * 3 + x, 2)]
+
+    def copy(ref, origin, out, into, peer):
+        return pltpu.make_async_remote_copy(
+            src_ref=ref, dst_ref=ref, send_sem=sems.at[out, origin], recv_sem=sems.at[into, origin],
+            device_id=peer, device_id_type=pl.DeviceIdType.MESH,
+        )
+
+    sent = []
+
+    def send(cond, *args):
+        pl.when(cond)(lambda: copy(*args).start())
+        sent.append((cond, args))
+
+    def arrive(cond, ref, origin, into):
+        pl.when(cond)(lambda: copy(ref, origin, 0, into, twin).wait_recv())
+
+    always = z >= 0
+    not_top, not_bottom = z < depth - 1, z > 0
+
+    def along(cond, origin, upward, downward):
+        if upward:
+            send(cond & not_top, s_ref.at[origin], origin, 0, 9, above)
+        if downward:
+            send(cond & not_bottom, s_ref.at[origin], origin, 1, 9, below)
+        send(cond, s_ref.at[origin], origin, 2, 9, beside)
+        if upward:
+            send(cond & not_top, plane_part(origin), origin, 3, 10, above)
+        if downward:
+            send(cond & not_bottom, plane_part(origin), origin, 4, 10, below)
+        send(cond, plane_part(origin), origin, 5, 10, beside)
+
+    def aside(cond, origin):
+        send(cond, w_ref.at[origin, core * 3 + 2 * x], origin, 6, 11, across)
+        send(cond, plane_part(origin), origin, 7, 12, twin)
+
+    others = []
+    along(always, tile, True, True)
+    for d in range(depth):
+        sides = [(always, z)] if d == 0 else [(z >= d, z - d), (z + d < depth, z + d)]
+        for k, (cond, zz) in enumerate(sides):
+            if d > 0:
+                origin = 2 * zz + y
+                arrive(cond, s_ref.at[origin], origin, 9)
+                arrive(cond, plane_part(origin), origin, 10)
+                along(cond, origin, k == 0, k == 1)
+                aside(cond, origin)
+                others.append((cond, origin))
+        for cond, zz in sides:
+            origin = 2 * zz + 1 - y
+            arrive(cond, s_ref.at[origin], origin, 9)
+            arrive(cond, plane_part(origin), origin, 10)
+            aside(cond, origin)
+            others.append((cond, origin))
+    for cond, origin in others:
+        part = w_ref.at[origin, core * 3 + 2 * (1 - x)]
+        arrive(cond, part, origin, 11)
+        send(cond, part, origin, 8, 13, twin)
+    for cond, origin in others:
+        arrive(cond, w_ref.at[origin, pl.ds((1 - core) * 3 + x, 2)], origin, 12)
+        arrive(cond, w_ref.at[origin, (1 - core) * 3 + 2 * (1 - x)], origin, 13)
+    for cond, args in sent:
+        pl.when(cond)(lambda args=args: copy(*args).wait_send())
+
+
 def classify_kernel(starts_ref, routes_ref, table_ref, weights_ref, out_ref):
-    slabs = weights_ref.shape[1]
-    stem_rows, expand_rows, shrink_rows = 512 // slabs, 256 // slabs, 1024 // slabs
-
     def rows_of(route, first, length):
-        return jnp.concatenate([weights_ref[route, s, first : first + length] for s in range(slabs)], axis=0)
+        return weights_ref[route, first : first + length]
 
     @pl.loop(0, out_ref.shape[0])
     def _(i):
@@ -98,35 +185,30 @@
             ],
             axis=0,
         )
-        stem = rows_of(route, 0, stem_rows)
+        stem = rows_of(route, 0, 512)
         hidden = jnp.dot(patches, stem, preferred_element_type=jnp.float32).astype(jnp.bfloat16)
         wide = hidden.astype(jnp.float32)
         scale = lax.rsqrt(jnp.mean(wide * wide, axis=1, keepdims=True) + 1e-05)
         normed = (wide * scale).astype(jnp.bfloat16)
         expanded = []
         for block in range(4):
-            expand = rows_of(route, stem_rows + block * expand_rows, expand_rows)
+            expand = rows_of(route, 512 + block * 256, 256)
             wider = jnp.dot(normed, expand, preferred_element_type=jnp.float32)
             expanded.append(jnp.maximum(wider, 0.0).astype(jnp.bfloat16))
-        shrink = rows_of(route, stem_rows + 4 * expand_rows, shrink_rows)
+        shrink = rows_of(route, 1536, 1024)
         added = jnp.dot(jnp.concatenate(expanded, axis=1), shrink, preferred_element_type=jnp.float32)
         last = (wide + added).astype(jnp.bfloat16).astype(jnp.float32)
-        head = weights_ref[route, 0, stem_rows + 4 * expand_rows + shrink_rows :].astype(jnp.float32)
+        head = rows_of(route, 2560, 16).astype(jnp.float32)
         total = head[0:8] * jnp.sum(last, axis=0, keepdims=True)
         score = jnp.sum(total, axis=1, keepdims=True) * (1.0 / patches.shape[0])
         out_ref[i] = jnp.broadcast_to(score, out_ref.shape[1:])
 
 
 def own_weights(stem_weight, expand_weight, shrink_weight, head_weight):
-    slabs, slab_me = lax.axis_size("slab"), lax.axis_index("slab")
-    stem, expand, shrink, head = stem_weight[0], expand_weight[0, 0], shrink_weight[0, 0], head_weight[0]
-    stem = lax.dynamic_slice_in_dim(stem.reshape(64, 8, 256), slab_me * (8 // slabs), 8 // slabs, axis=1)
-    stem = stem.transpose(1, 0, 2).reshape(512 // slabs, 256)
-    expand = lax.dynamic_slice_in_dim(expand, slab_me * (256 // slabs), 256 // slabs, axis=0)
-    expand = [expand[:, 256 * m : 256 * m + 256] for m in range(4)]
-    shrink = lax.dynamic_slice_in_dim(shrink, slab_me * (1024 // slabs), 1024 // slabs, axis=0)
-    head = jnp.pad(head.T, ((0, 8), (0, 0)))
-    return jnp.concatenate([stem] + expand + [shrink, head], axis=0)
+    stem = stem_weight[0].reshape(64, 8, 256).transpose(1, 0, 2).reshape(512, 256)
+    expand = [expand_weight[0, 0][:, 256 * m : 256 * m + 256] for m in range(4)]
+    head = jnp.pad(head_weight[0].T, ((0, 24), (0, 0)))
+    return jnp.concatenate([stem] + expand + [shrink_weight[0, 0], head], axis=0)
 
 
 def body(
@@ -151,13 +233,32 @@
     after = lax.ppermute(raw[:HALO], "slab", down)
     raw = jnp.concatenate([before, raw, after], axis=0)
     deep = planes + 2 * HALO
-    strips = lax.all_gather(raw[:, :, :OV], "tile", axis=0)
-
+    strip = raw[:, :, :OV].reshape(deep, rows * OV // 128, 128)
     share = own_weights(stem_weight, expand_weight, shrink_weight, head_weight)
-    weights = lax.all_gather(share, ("tile", "slab"), axis=0)
-    weights = weights.reshape(tiles, slabs, share.shape[0], 256)
+    if tiles == 8 and slabs == 4:
+        share = share.reshape(6, share.shape[0] // 6, 256)
+        anywhere = pl.BlockSpec(memory_space=pl.ANY)
+        weights, strips = pl.pallas_call(
+            gather_kernel,
+            out_shape=(
+                jax.ShapeDtypeStruct((tiles,) + share.shape, share.dtype),
+                jax.ShapeDtypeStruct((tiles,) + strip.shape, strip.dtype),
+            ),
+            in_specs=[anywhere, anywhere],
+            out_specs=(anywhere, anywhere),
+            scratch_shapes=[pltpu.SemaphoreType.DMA((14, tiles)), pltpu.SemaphoreType.DMA((2,))],
+            compiler_params=pltpu.CompilerParams(collective_id=0, has_side_effects=True),
+            name="gather",
+        )(share, strip)
+    else:
+        strips = lax.all_gather(strip, "tile", axis=0)
+        part = share.shape[0] // slabs
+        share = lax.dynamic_slice_in_dim(share, slab_me * part, part, axis=0)
+        weights = lax.all_gather(share, ("tile", "slab"), axis=0)
+    weights = weights.reshape(tiles, -1, 256)
 
     mate = lax.dynamic_index_in_dim(strips, partner[tile_me], 0, keepdims=False)
+    mate = mate.reshape(deep, rows, OV)
     mate = lax.dynamic_slice_in_dim(
         jnp.concatenate([mate, mate], axis=1), rows - offsets[tile_me], rows, axis=1
     ).astype(jnp.float32)

time: 139 us -> 169 us (1.22)
  Pallas kernels: 31.2 us -> 150 us
  blocking collectives: 45.7 us -> 0 us
  waiting for transfers between devices: 29.4 us -> 0.01 us
  between operations: 17.4 us -> 4.06 us
    pallas_call x0 -> x1, Pallas kernels: none -> 118 us  [body(): pl.pallas_call(gather_kernel, out_shape=(jax.ShapeDtypeStruct((tiles,) +...]
    all_gather x1 -> x0, blocking collectives: 45.7 us -> none  [body(): strips = lax.all_gather(raw[:, :, :OV], 'tile', axis=0)]
    all_gather x1 -> x0, waiting for transfers between devices: 29.4 us -> none  [body(): weights = lax.all_gather(share, ('tile', 'slab'), axis=0)]
    unnamed x23 -> x22, local copies, waits for them, and re-layouts: 3.24 us -> 0.62 us
  transfers between devices with their start and end apart: 3 -> 2, of which waited for: 1 -> 0; matrix products, arithmetic and copies ran while one was open for 3% -> 2% of each run, Pallas kernels for 9% -> 0%
where the time goes in v2:
time: 169 us; the launch traced here: 167 us
  Pallas kernels  150 us (89%)
  local copies, waits for them, and re-layouts  7.24 us (4%)
  between operations  4.06 us (2%)
  starting transfers between devices  3.66 us (2%)
  other arithmetic  2.29 us (1%)
    pallas_call x1, Pallas kernels, body(): pl.pallas_call(gather_kernel, out_shape=(jax.ShapeDtypeStruct((tiles,) +...  118 us
    pallas_call x1, Pallas kernels, body(): pl.pallas_call(classify_kernel, out_shape=jax.ShapeDtypeStruct((count, 8,...  18.9 us
    pallas_call x1, Pallas kernels, body(): pl.pallas_call(band_kernel, out_shape=(jax.ShapeDtypeStruct((planes, rows...  12.2 us
  transfers between devices with their start and end apart: 2, of which 0 were waited for; matrix products, arithmetic and copies ran while one was open for 2% of the time, Pallas kernels for 0%

profile of v2, /device:TPU:0, one launch (start us, length us, event | category | flops | bytes accessed | tf_op | source)
XLA Modules:
  0.0 166.9 jit_solution(11940243314020772410)
XLA Ops:
  0.6 0.0 copy-start.3
  0.6 0.0 copy-start.4
  0.6 1.1 slice_bitcast_fusion.1
  1.7 2.4 %collective-permute-start = (bf16[4,64,256]{2,1,0:T(8,128)(2,1)S(1)}, bf16[4,64,256]{2,1,0:T(8,128)(2,1)S(1)}, u32[]{:S(2)}, u32[]{:S(2)}) collective-permute-start(bf16[4,64,256]{2,1,0:T(8,128)(2,1)S(1)} %get-tuple-element.12), channel_id=1, source_target_pairs={{0,1},{1,2},{2,3},{4,5},{5,6},{6,7},{8,9},{9,10},{10,11},{12,13},{... | collective-permute-start | bytes 393224 | tf_op jit(solution)/shard_map/ppermute | solution.py:232
  4.1 1.3 collective-permute-start.1
  5.4 1.0 copy.20
  6.4 0.0 copy-start.5
  6.4 0.0 copy-start.6
  6.4 0.0 copy-start.7
  6.5 0.0 copy-done.3
  6.6 0.0 copy-done.4
  6.7 0.4 copy-done.5
  7.1 0.0 copy-start.2
  7.1 0.1 add_convert_fusion.flags_ref
  7.2 0.0 copy-done.6
  7.2 0.7 dynamic_slice.13
  9.2 0.0 copy-done.7
  9.2 0.6 dynamic_slice.15
  11.7 0.1 select_add_fusion.band_ref
  11.8 0.0 collective-permute-done
  11.8 0.0 collective-permute-done.1
  11.8 1.2 pad_maximum_fusion.1
  13.1 0.0 copy-done.2
  13.1 0.1 slice.53
  13.1 0.9 reshape.37.own_s
  14.0 118.5 %gather.1 = (bf16[8,6,432,256]{3,2,1,0:T(8,128)(2,1)}, bf16[8,24,16,128]{3,2,1,0:T(8,128)(2,1)}) custom-call(bf16[6,432,256]{2,1,0:T(8,128)(2,1)} %bitcast.30, bf16[24,16,128]{2,1,0:T(8,128)(2,1)} %reshape.37.own_s), custom_call_target="tpu_custom_call" | custom-call | tf_op jit(solution)/shard_map/gather/pallas_call | solution.py:241
  132.5 0.9 constant_dynamic-slice_fusion
  133.4 0.2 reshape.38
  133.6 0.5 slice.54
  134.1 0.4 fusion
  134.5 0.5 pad_maximum_fusion.joined_ref
  135.0 0.0 copy-start
  135.0 0.0 copy-start.1
  135.0 12.2 %band.1 = (f32[16,64,256]{2,1,0:T(8,128)}, bf16[256,32,128]{2,1,0:T(8,128)(2,1)S(1)}) custom-call(f32[2]{0:T(128)S(1)} %add_convert_fusion.flags_ref, f32[24,64,256]{2,1,0:T(8,128)S(1)} %pad_maximum_fusion.joined_ref, f32[256,256]{1,0:T(8,128)S(1)} %select_add_fusion.band_ref), custom_call_target="tpu_custom_call" | custom-call | flops 1000000000 | bytes 6000000 | tf_op jit(solution)/shard_map/band/pallas_call | solution.py:278
  147.3 0.0 copy-done
  147.3 0.0 copy-done.1
  147.3 18.9 %classify.1 = f32[16,8,128]{2,1,0:T(8,128)S(1)} custom-call(s32[16]{0:T(128)S(1)} %copy-done, s32[16]{0:T(128)S(1)} %bitcast.29, bf16[256,32,128]{2,1,0:T(8,128)(2,1)S(1)} %get-tuple-element.8.table_ref, bf16[8,2592,256]{2,1,0:T(8,128)(2,1)} %bitcast.40), custom_call_target="tpu_custom_call" | custom-call | flops 5400000000 | bytes 13000000 | tf_op jit(solution)/shard_map/classify/pallas_call | solution.py:297
  166.2 0.7 copy.21
  (8 shorter events, 0.1 us)
Async XLA Ops:
  0.6 5.9 %copy-start.3 = (bf16[1,1,256,1024]{3,2,1,0:T(8,128)(2,1)S(1)}, bf16[1,1,256,1024]{3,2,1,0:T(8,128)(2,1)}, u32[]{:S(2)}) copy-start(bf16[1,1,256,1024]{3,2,1,0:T(8,128)(2,1)} %param.15) | copy-start | bytes 1572868
  0.6 6.0 %copy-start.4 = (bf16[1,1,1024,256]{3,2,1,0:T(8,128)(2,1)S(1)}, bf16[1,1,1024,256]{3,2,1,0:T(8,128)(2,1)}, u32[]{:S(2)}) copy-start(bf16[1,1,1024,256]{3,2,1,0:T(8,128)(2,1)} %param.16) | copy-start | bytes 1572868
  1.7 10.1 %collective-permute-start = (bf16[4,64,256]{2,1,0:T(8,128)(2,1)S(1)}, bf16[4,64,256]{2,1,0:T(8,128)(2,1)S(1)}, u32[]{:S(2)}, u32[]{:S(2)}) collective-permute-start(bf16[4,64,256]{2,1,0:T(8,128)(2,1)S(1)} %get-tuple-element.12), channel_id=1, source_target_pairs={{0,1},{1,2},{2,3},{4,5},{5,6},{6,7},{8,9},{9,10},{10,11},{12,13},{... | collective-permute-start | bytes 393224 | tf_op jit(solution)/shard_map/ppermute | solution.py:232
  4.1 7.7 %collective-permute-start.1 = (bf16[4,64,256]{2,1,0:T(8,128)(2,1)S(1)}, bf16[4,64,256]{2,1,0:T(8,128)(2,1)S(1)}, u32[]{:S(2)}, u32[]{:S(2)}) collective-permute-start(bf16[4,64,256]{2,1,0:T(8,128)(2,1)S(1)} %get-tuple-element.13), channel_id=1, source_target_pairs={{1,0},{2,1},{3,2},{5,4},{6,5},{7,6},{9,8},{10,9},{11,10},{13,12},{... | collective-permute-start | bytes 393224 | tf_op jit(solution)/shard_map/ppermute | solution.py:233
  6.4 0.7 copy-start.5
  6.4 0.8 copy-start.6
  6.4 2.7 %copy-start.7 = (s32[8]{0:T(128)S(1)}, s32[8]{0:T(128)}, u32[]{:S(2)}) copy-start(s32[8]{0:T(128)} %param.11) | copy-start | bytes 100
  7.1 5.9 %copy-start.2 = (bf16[2592,256]{1,0:T(8,128)(2,1)}, bf16[2592,256]{1,0:T(8,128)(2,1)S(1)}, u32[]{:S(2)}) copy-start(bf16[2592,256]{1,0:T(8,128)(2,1)S(1)} %constant_dynamic-update-slice_fusion) | copy-start | bytes 3981316
  135.0 12.3 %copy-start = (s32[16]{0:T(128)S(1)}, s32[16]{0:T(128)}, u32[]{:S(2)}) copy-start(s32[16]{0:T(128)} %starts_ref.1) | copy-start | bytes 196
  135.0 12.3 %copy-start.1 = (s32[16,1]{0,1:T(1,128)S(1)}, s32[16,1]{0,1:T(1,128)}, u32[]{:S(2)}) copy-start(s32[16,1]{0,1:T(1,128)} %param.13) | copy-start | bytes 196

commit v3 on v1

--- a/solution.py
+++ b/solution.py
@@ -80,6 +80,60 @@
             table_ref[x] = turned[pl.ds(x, spots, stride=pitch), :].astype(jnp.bfloat16)
 
 
+def strip_kernel(own_ref, strips_ref, sems, local):
+    tile, slab = lax.axis_index("tile"), lax.axis_index("slab")
+    depth = lax.axis_size("tile") // 2
+    z, y = tile // 2, tile % 2
+    above, below, beside = (tile + 2, slab), (tile - 2, slab), (2 * z + 1 - y, slab)
+    not_top, not_bottom = z < depth - 1, z > 0
+    own = pltpu.make_async_copy(own_ref, strips_ref.at[tile], local)
+    own.start()
+    barrier = pltpu.get_barrier_semaphore()
+
+    def greet(peer):
+        pl.semaphore_signal(barrier, inc=1, device_id=peer, device_id_type=pl.DeviceIdType.MESH)
+
+    greet(beside)
+    pl.when(not_top)(lambda: greet(above))
+    pl.when(not_bottom)(lambda: greet(below))
+    ends = jnp.where(z == 0, 1, 0) + jnp.where(z == depth - 1, 1, 0)
+    pl.semaphore_wait(barrier, 3 - ends)
+    own.wait()
+    sent = []
+
+    def copy(origin, out, peer):
+        return pltpu.make_async_remote_copy(
+            src_ref=strips_ref.at[origin], dst_ref=strips_ref.at[origin],
+            send_sem=sems.at[out, origin], recv_sem=sems.at[3, origin],
+            device_id=peer, device_id_type=pl.DeviceIdType.MESH,
+        )
+
+    def send(cond, *args):
+        pl.when(cond)(lambda: copy(*args).start())
+        sent.append((cond, args))
+
+    def arrive(cond, origin):
+        pl.when(cond)(lambda: copy(origin, 0, beside).wait_recv())
+
+    send(not_top, tile, 0, above)
+    send(not_bottom, tile, 1, below)
+    send(z >= 0, tile, 2, beside)
+    for d in range(1, depth):
+        for cond, origin, more, out, onward in (
+            (z >= d, tile - 2 * d, not_top, 0, above),
+            (z + d < depth, tile + 2 * d, not_bottom, 1, below),
+        ):
+            arrive(cond, origin)
+            send(cond & more, origin, out, onward)
+            send(cond, origin, 2, beside)
+    arrive(z >= 0, 2 * z + 1 - y)
+    for d in range(1, depth):
+        arrive(z >= d, 2 * (z - d) + 1 - y)
+        arrive(z + d < depth, 2 * (z + d) + 1 - y)
+    for cond, args in sent:
+        pl.when(cond)(lambda args=args: copy(*args).wait_send())
+
+
 def classify_kernel(starts_ref, routes_ref, table_ref, weights_ref, out_ref):
     slabs = weights_ref.shape[1]
     stem_rows, expand_rows, shrink_rows = 512 // slabs, 256 // slabs, 1024 // slabs
@@ -87,7 +141,7 @@
     def rows_of(route, first, length):
         return jnp.concatenate([weights_ref[route, s, first : first + length] for s in range(slabs)], axis=0)
 
-    @pl.loop(0, out_ref.shape[0])
+    @pl.loop(0, out_ref.shape[0], unroll=2)
     def _(i):
         start = starts_ref[i]
         route = routes_ref[i]
@@ -151,13 +205,28 @@
     after = lax.ppermute(raw[:HALO], "slab", down)
     raw = jnp.concatenate([before, raw, after], axis=0)
     deep = planes + 2 * HALO
-    strips = lax.all_gather(raw[:, :, :OV], "tile", axis=0)
+    strip = raw[:, :, :OV].reshape(deep, rows * OV // 128, 128)
+    if tiles == 8 and slabs == 4:
+        anywhere = pl.BlockSpec(memory_space=pl.ANY)
+        strips = pl.pallas_call(
+            strip_kernel,
+            out_shape=jax.ShapeDtypeStruct((tiles,) + strip.shape, strip.dtype),
+            in_specs=[anywhere],
+            out_specs=anywhere,
+            scratch_shapes=[pltpu.SemaphoreType.DMA((4, tiles)), pltpu.SemaphoreType.DMA],
+            compiler_params=pltpu.CompilerParams(collective_id=0, has_side_effects=True),
+            cost_estimate=pl.CostEstimate(flops=0, bytes_accessed=40 * 10**6, transcendentals=0),
+            name="strips",
+        )(strip)
+    else:
+        strips = lax.all_gather(strip, "tile", axis=0)
 
     share = own_weights(stem_weight, expand_weight, shrink_weight, head_weight)
     weights = lax.all_gather(share, ("tile", "slab"), axis=0)
     weights = weights.reshape(tiles, slabs, share.shape[0], 256)
 
     mate = lax.dynamic_index_in_dim(strips, partner[tile_me], 0, keepdims=False)
+    mate = mate.reshape(deep, rows, OV)
     mate = lax.dynamic_slice_in_dim(
         jnp.concatenate([mate, mate], axis=1), rows - offsets[tile_me], rows, axis=1
     ).astype(jnp.float32)

time: 139 us -> 126 us (0.906)
  blocking collectives: 45.7 us -> 0 us
  Pallas kernels: 31.2 us -> 59.1 us
  waiting for transfers between devices: 29.4 us -> 33.5 us
    all_gather x1 -> x0, blocking collectives: 45.7 us -> none  [body(): strips = lax.all_gather(raw[:, :, :OV], 'tile', axis=0)]
    pallas_call x0 -> x1, Pallas kernels: none -> 31.3 us  [body(): pl.pallas_call(strip_kernel, out_shape=jax.ShapeDtypeStruct((tiles,) + st...]
    all_gather x1, waiting for transfers between devices: 29.4 us -> 33.5 us  [body(): weights = lax.all_gather(share, ('tile', 'slab'), axis=0)]
    pallas_call x1, Pallas kernels: 19 us -> 15.6 us  [body(): pl.pallas_call(classify_kernel, out_shape=jax.ShapeDtypeStruct((count, 8,...]
    unnamed x23 -> x22, local copies, waits for them, and re-layouts: 3.24 us -> 2.72 us
  transfers between devices with their start and end apart: 3 -> 3, of which waited for: 1 -> 1; matrix products, arithmetic and copies ran while one was open for 3% -> 5% of each run, Pallas kernels for 9% -> 35%
where the time goes in v3:
time: 126 us
  Pallas kernels  59.1 us (47%)
  waiting for transfers between devices  33.5 us (27%)
  between operations  17.4 us (14%)
  local copies, waits for them, and re-layouts  10.1 us (8%)
  starting transfers between devices  4.37 us (3%)
    all_gather x1, waiting for transfers between devices, body(): weights = lax.all_gather(share, ('tile', 'slab'), axis=0)  33.5 us
    pallas_call x1, Pallas kernels, body(): pl.pallas_call(strip_kernel, out_shape=jax.ShapeDtypeStruct((tiles,) + st...  31.3 us
    pallas_call x1, Pallas kernels, body(): pl.pallas_call(classify_kernel, out_shape=jax.ShapeDtypeStruct((count, 8,...  15.6 us
    pallas_call x1, Pallas kernels, body(): pl.pallas_call(band_kernel, out_shape=(jax.ShapeDtypeStruct((planes, rows...  12.2 us
    ppermute x1, starting transfers between devices, body(): before = lax.ppermute(raw[planes - HALO:], 'slab', up)  3.04 us
    unnamed x22, local copies, waits for them, and re-layouts  2.72 us
  transfers between devices with their start and end apart: 3, of which 1 were waited for; matrix products, arithmetic and copies ran while one was open for 5% of the time, Pallas kernels for 35%

profile of v3, /device:TPU:0, one launch (start us, length us, event | category | flops | bytes accessed | tf_op | source)
XLA Modules:
  0.0 125.8 jit_solution(526056143211902620)
XLA Ops:
  7.2 0.0 copy-start
  7.2 0.0 copy-start.4
  7.2 0.0 copy-start.6
  7.2 0.0 copy-start.7
  7.2 0.0 all-gather.3.cloned.1.call-start
  7.3 1.1 dynamic-slice_bitcast_fusion.1
  8.4 0.0 copy-done
  8.5 0.9 bitcast_dynamic-update-slice_fusion
  9.4 0.7 constant_dynamic-update-slice_fusion
  10.1 0.0 copy-start.5
  10.1 0.7 copy-done.5
  10.9 0.0 all-gather.3.cloned.1.call-update
  10.9 0.0 copy-done.4
  10.9 1.3 %collective-permute-start.1 = (bf16[4,64,256]{2,1,0:T(8,128)(2,1)S(1)}, bf16[4,64,256]{2,1,0:T(8,128)(2,1)S(1)}, u32[]{:S(2)}, u32[]{:S(2)}) collective-permute-start(bf16[4,64,256]{2,1,0:T(8,128)(2,1)S(1)} %get-tuple-element.9), channel_id=1, source_target_pairs={{1,0},{2,1},{3,2},{5,4},{6,5},{7,6},{9,8},{10,9},{11,10},{13,12},{... | collective-permute-start | bytes 393224 | tf_op jit(solution)/shard_map/ppermute | solution.py:205
  12.2 3.0 %collective-permute-start = (bf16[4,64,256]{2,1,0:T(8,128)(2,1)S(1)}, bf16[4,64,256]{2,1,0:T(8,128)(2,1)S(1)}, u32[]{:S(2)}, u32[]{:S(2)}) collective-permute-start(bf16[4,64,256]{2,1,0:T(8,128)(2,1)S(1)} %get-tuple-element.8), channel_id=1, source_target_pairs={{0,1},{1,2},{2,3},{4,5},{5,6},{6,7},{8,9},{9,10},{10,11},{12,13},{... | collective-permute-start | bytes 393224 | tf_op jit(solution)/shard_map/ppermute | solution.py:204
  15.3 0.1 add_convert_fusion.flags_ref
  15.4 0.0 copy-done.6
  15.4 0.6 dynamic_slice.26
  17.2 0.0 copy-done.7
  17.2 0.6 dynamic_slice.28
  19.7 0.1 select_add_fusion.band_ref
  19.8 0.0 collective-permute-done.1
  19.8 0.0 collective-permute-done
  19.9 0.2 pad_maximum_fusion.1
  20.0 1.6 %slice.50 = f32[24,64,224]{2,1,0:T(8,128)} slice(f32[24,64,256]{2,1,0:T(8,128)S(1)} %get-tuple-element.7), slice={[0:24], [0:64], [32:256]} | slice | bytes 2752512 | tf_op jit(solution)/shard_map/slice | solution.py:236
  21.6 0.1 slice.49
  21.7 0.9 reshape.34.own_ref
  22.6 31.3 %strips.1 = bf16[8,24,16,128]{3,2,1,0:T(8,128)(2,1)} custom-call(bf16[24,16,128]{2,1,0:T(8,128)(2,1)} %reshape.34.own_ref), custom_call_target="tpu_custom_call" | custom-call | bytes 40000000 | tf_op jit(solution)/shard_map/strips/pallas_call | solution.py:211
  53.9 0.9 constant_dynamic-slice_fusion
  54.8 0.2 reshape.35
  55.0 0.0 copy-start.3
  55.0 0.4 fusion
  55.4 1.0 copy-done.3
  56.4 0.5 pad_maximum_fusion.joined_ref
  56.9 0.0 copy-start.1
  56.9 0.0 copy-start.2
  56.9 12.2 %band.1 = (f32[16,64,256]{2,1,0:T(8,128)}, bf16[256,32,128]{2,1,0:T(8,128)(2,1)S(1)}) custom-call(f32[2]{0:T(128)S(1)} %add_convert_fusion.flags_ref, f32[24,64,256]{2,1,0:T(8,128)S(1)} %pad_maximum_fusion.joined_ref, f32[256,256]{1,0:T(8,128)S(1)} %select_add_fusion.band_ref), custom_call_target="tpu_custom_call" | custom-call | flops 1000000000 | bytes 6000000 | tf_op jit(solution)/shard_map/band/pallas_call | solution.py:246
  69.1 33.5 %all-gather.3.cloned.1.call-done = bf16[20992,256]{1,0:T(8,128)(2,1)} async-done(((bf16[656,256]{1,0:T(8,128)(2,1)}), bf16[20992,256]{1,0:T(8,128)(2,1)}) %all-gather.3.cloned.1.call-update) | async-done | bytes 10747920 | tf_op jit(solution)/shard_map/all_gather | solution.py:225
  102.6 0.0 copy-done.1
  102.6 0.0 copy-done.2
  102.6 15.6 %classify.1 = f32[16,8,128]{2,1,0:T(8,128)S(1)} custom-call(s32[16]{0:T(128)S(1)} %copy-done.1, s32[16]{0:T(128)S(1)} %bitcast.29, bf16[256,32,128]{2,1,0:T(8,128)(2,1)S(1)} %get-tuple-element.5.table_ref, bf16[8,4,656,256]{3,2,1,0:T(8,128)(2,1)} %bitcast.35), custom_call_target="tpu_custom_call" | custom-call | flops 5400000000 | bytes 13000000 | tf_op jit(solution)/shard_map/classify/pallas_call | solution.py:265
  118.2 0.7 copy.21
  (9 shorter events, 0.1 us)
Async XLA Ops:
  7.2 1.2 copy-start
  7.2 3.7 %copy-start.4 = (bf16[1,16,64,256]{3,2,1,0:T(8,128)(2,1)S(1)}, bf16[1,16,64,256]{3,2,1,0:T(8,128)(2,1)}, u32[]{:S(2)}) copy-start(bf16[1,16,64,256]{3,2,1,0:T(8,128)(2,1)} %param.9) | copy-start | bytes 1572868
  7.2 8.2 %copy-start.6 = (s32[8]{0:T(128)S(1)}, s32[8]{0:T(128)}, u32[]{:S(2)}) copy-start(s32[8]{0:T(128)} %param.10) | copy-start | bytes 100
  7.2 10.0 %copy-start.7 = (s32[8]{0:T(128)S(1)}, s32[8]{0:T(128)}, u32[]{:S(2)}) copy-start(s32[8]{0:T(128)} %param.11) | copy-start | bytes 100
  7.2 95.4 %all-gather.3.cloned.1.call-start = ((), (), s32[]{:S(2)}) async-start(), calls=%async_computation | async-start | bytes 11083776 | tf_op jit(solution)/shard_map/all_gather | solution.py:225
  10.1 0.7 copy-start.5
  10.9 8.9 %collective-permute-start.1 = (bf16[4,64,256]{2,1,0:T(8,128)(2,1)S(1)}, bf16[4,64,256]{2,1,0:T(8,128)(2,1)S(1)}, u32[]{:S(2)}, u32[]{:S(2)}) collective-permute-start(bf16[4,64,256]{2,1,0:T(8,128)(2,1)S(1)} %get-tuple-element.9), channel_id=1, source_target_pairs={{1,0},{2,1},{3,2},{5,4},{6,5},{7,6},{9,8},{10,9},{11,10},{13,12},{... | collective-permute-start | bytes 393224 | tf_op jit(solution)/shard_map/ppermute | solution.py:205
  12.2 7.6 %collective-permute-start = (bf16[4,64,256]{2,1,0:T(8,128)(2,1)S(1)}, bf16[4,64,256]{2,1,0:T(8,128)(2,1)S(1)}, u32[]{:S(2)}, u32[]{:S(2)}) collective-permute-start(bf16[4,64,256]{2,1,0:T(8,128)(2,1)S(1)} %get-tuple-element.8), channel_id=1, source_target_pairs={{0,1},{1,2},{2,3},{4,5},{5,6},{6,7},{8,9},{9,10},{10,11},{12,13},{... | collective-permute-start | bytes 393224 | tf_op jit(solution)/shard_map/ppermute | solution.py:204
  55.0 1.4 %copy-start.3 = (f32[24,64,224]{2,1,0:T(8,128)S(1)}, f32[24,64,224]{2,1,0:T(8,128)}, u32[]{:S(2)}) copy-start(f32[24,64,224]{2,1,0:T(8,128)} %slice.50) | copy-start | bytes 4128772
  56.9 45.7 %copy-start.1 = (s32[16]{0:T(128)S(1)}, s32[16]{0:T(128)}, u32[]{:S(2)}) copy-start(s32[16]{0:T(128)} %starts_ref.1) | copy-start | bytes 196
  56.9 45.7 %copy-start.2 = (s32[16,1]{0,1:T(1,128)S(1)}, s32[16,1]{0,1:T(1,128)}, u32[]{:S(2)}) copy-start(s32[16,1]{0,1:T(1,128)} %param.13) | copy-start | bytes 196
Sparse Core Ops, SparseCore 0:
  11.0 91.5 all-gather.2

commit v4 on v3

--- a/solution.py
+++ b/solution.py
@@ -9,6 +9,7 @@
 from jax.sharding import PartitionSpec as P
 
 OV = 32
+CX = 64
 RADIUS = 3
 HALO = RADIUS + 1
 PAD = 8
@@ -134,41 +135,44 @@
         pl.when(cond)(lambda args=args: copy(*args).wait_send())
 
 
-def classify_kernel(starts_ref, routes_ref, table_ref, weights_ref, out_ref):
+def rows_of(ref, route, first, length):
+    return jnp.concatenate([ref[route, s, first : first + length] for s in range(ref.shape[1])], axis=0)
+
+
+def expand_kernel(starts_ref, routes_ref, table_ref, weights_ref, hidden_ref, expanded_ref):
     slabs = weights_ref.shape[1]
-    stem_rows, expand_rows, shrink_rows = 512 // slabs, 256 // slabs, 1024 // slabs
-
-    def rows_of(route, first, length):
-        return jnp.concatenate([weights_ref[route, s, first : first + length] for s in range(slabs)], axis=0)
-
-    @pl.loop(0, out_ref.shape[0], unroll=2)
-    def _(i):
-        start = starts_ref[i]
-        route = routes_ref[i]
-        patches = jnp.concatenate(
-            [
-                jnp.concatenate([table_ref[start + 8 * c + 2 * j] for j in range(4)], axis=1)
-                for c in range(8)
-            ],
-            axis=0,
-        )
-        stem = rows_of(route, 0, stem_rows)
-        hidden = jnp.dot(patches, stem, preferred_element_type=jnp.float32).astype(jnp.bfloat16)
-        wide = hidden.astype(jnp.float32)
-        scale = lax.rsqrt(jnp.mean(wide * wide, axis=1, keepdims=True) + 1e-05)
-        normed = (wide * scale).astype(jnp.bfloat16)
-        expanded = []
-        for block in range(4):
-            expand = rows_of(route, stem_rows + block * expand_rows, expand_rows)
-            wider = jnp.dot(normed, expand, preferred_element_type=jnp.float32)
-            expanded.append(jnp.maximum(wider, 0.0).astype(jnp.bfloat16))
-        shrink = rows_of(route, stem_rows + 4 * expand_rows, shrink_rows)
-        added = jnp.dot(jnp.concatenate(expanded, axis=1), shrink, preferred_element_type=jnp.float32)
-        last = (wide + added).astype(jnp.bfloat16).astype(jnp.float32)
-        head = weights_ref[route, 0, stem_rows + 4 * expand_rows + shrink_rows :].astype(jnp.float32)
-        total = head[0:8] * jnp.sum(last, axis=0, keepdims=True)
-        score = jnp.sum(total, axis=1, keepdims=True) * (1.0 / patches.shape[0])
-        out_ref[i] = jnp.broadcast_to(score, out_ref.shape[1:])
+    stem_rows, expand_rows = 512 // slabs, 256 // slabs
+    start = starts_ref[pl.program_id(0)]
+    route = routes_ref[pl.program_id(0)]
+    patches = jnp.concatenate(
+        [
+            jnp.concatenate([table_ref[start + 8 * c + 2 * j] for j in range(4)], axis=1)
+            for c in range(8)
+        ],
+        axis=0,
+    )
+    stem = rows_of(weights_ref, route, 0, stem_rows)
+    hidden = jnp.dot(patches, stem, preferred_element_type=jnp.float32).astype(jnp.bfloat16)
+    hidden_ref[0] = hidden
+    wide = hidden.astype(jnp.float32)
+    scale = lax.rsqrt(jnp.mean(wide * wide, axis=1, keepdims=True) + 1e-05)
+    normed = (wide * scale).astype(jnp.bfloat16)
+    for block in range(4):
+        expand = rows_of(weights_ref, route, stem_rows + block * expand_rows, expand_rows)
+        wider = jnp.dot(normed, expand, preferred_element_type=jnp.float32)
+        expanded_ref[0, :, 256 * block : 256 * block + 256] = jnp.maximum(wider, 0.0).astype(jnp.bfloat16)
+
+
+def shrink_kernel(routes_ref, hidden_ref, expanded_ref, weights_ref, out_ref):
+    route = routes_ref[pl.program_id(0)]
+    shrink_rows = 1024 // weights_ref.shape[1]
+    shrink = rows_of(weights_ref, route, 0, shrink_rows)
+    added = jnp.dot(expanded_ref[0], shrink, preferred_element_type=jnp.float32)
+    last = (hidden_ref[0].astype(jnp.float32) + added).astype(jnp.bfloat16).astype(jnp.float32)
+    head = weights_ref[route, 0, shrink_rows:].astype(jnp.float32)
+    total = head[0:8] * jnp.sum(last, axis=0, keepdims=True)
+    score = jnp.sum(total, axis=1, keepdims=True) * (1.0 / last.shape[0])
+    out_ref[0] = jnp.broadcast_to(score, out_ref.shape[1:])
 
 
 def own_weights(stem_weight, expand_weight, shrink_weight, head_weight):
@@ -180,7 +184,7 @@
     expand = [expand[:, 256 * m : 256 * m + 256] for m in range(4)]
     shrink = lax.dynamic_slice_in_dim(shrink, slab_me * (1024 // slabs), 1024 // slabs, axis=0)
     head = jnp.pad(head.T, ((0, 8), (0, 0)))
-    return jnp.concatenate([stem] + expand + [shrink, head], axis=0)
+    return jnp.concatenate([stem] + expand, axis=0), jnp.concatenate([shrink, head], axis=0)
 
 
 def body(
@@ -221,9 +225,10 @@
     else:
         strips = lax.all_gather(strip, "tile", axis=0)
 
-    share = own_weights(stem_weight, expand_weight, shrink_weight, head_weight)
-    weights = lax.all_gather(share, ("tile", "slab"), axis=0)
-    weights = weights.reshape(tiles, slabs, share.shape[0], 256)
+    shares = own_weights(stem_weight, expand_weight, shrink_weight, head_weight)
+    early, late = [
+        lax.all_gather(share, ("tile", "slab"), axis=0).reshape((tiles, slabs) + share.shape) for share in shares
+    ]
 
     mate = lax.dynamic_index_in_dim(strips, partner[tile_me], 0, keepdims=False)
     mate = mate.reshape(deep, rows, OV)
@@ -262,15 +267,35 @@
     )(flags, joined, band)
 
     count = starts.shape[0]
+    routes = classifier[:, 0]
+    spots_all = rows * planes * CX // 256
+
+    def one(*shape):
+        return pl.BlockSpec((1,) + shape, lambda i: (i, 0, 0))
+
+    hidden, expanded = pl.pallas_call(
+        expand_kernel,
+        grid=(count,),
+        out_shape=(
+            jax.ShapeDtypeStruct((count, spots_all, 256), jnp.bfloat16),
+            jax.ShapeDtypeStruct((count, spots_all, 1024), jnp.bfloat16),
+        ),
+        in_specs=[smem, smem, vmem, vmem],
+        out_specs=(one(spots_all, 256), one(spots_all, 1024)),
+        compiler_params=pltpu.CompilerParams(vmem_limit_bytes=48 * 1024 * 1024),
+        cost_estimate=pl.CostEstimate(flops=32 * 10**8, bytes_accessed=20 * 10**6, transcendentals=0),
+        name="expand",
+    )(starts, routes, table, early)
     scores = pl.pallas_call(
-        classify_kernel,
+        shrink_kernel,
+        grid=(count,),
         out_shape=jax.ShapeDtypeStruct((count, 8, 128), jnp.float32),
-        in_specs=[smem, smem, vmem, vmem],
-        out_specs=vmem,
+        in_specs=[smem, one(spots_all, 256), one(spots_all, 1024), vmem],
+        out_specs=one(8, 128),
         compiler_params=pltpu.CompilerParams(vmem_limit_bytes=48 * 1024 * 1024),
-        cost_estimate=pl.CostEstimate(flops=54 * 10**8, bytes_accessed=13 * 10**6, transcendentals=0),
-        name="classify",
-    )(starts, classifier[:, 0], table, weights)
+        cost_estimate=pl.CostEstimate(flops=21 * 10**8, bytes_accessed=15 * 10**6, transcendentals=0),
+        name="shrink",
+    )(routes, hidden, expanded, late)
     return log_response[None], scores[:, :, 0]
 
 

time: 126 us -> 170 us (1.35)
  waiting for transfers between devices: 33.5 us -> 61.7 us
  Pallas kernels: 59.1 us -> 70.7 us
  local copies, waits for them, and re-layouts: 10.1 us -> 12.3 us
    all_gather x1 -> x2, waiting for transfers between devices: 33.5 us -> 61.7 us  [body(): lax.all_gather(share, ('tile', 'slab'), axis=0)]
    pallas_call x1 -> x2, Pallas kernels: 15.6 us -> 28.9 us  [the longest x1 15.3 us: body(): pl.pallas_call(expand_kernel, grid=(count,), out_shape=(jax.ShapeDtypeStr...]
    unnamed x22 -> x24, local copies, waits for them, and re-layouts: 2.72 us -> 4.64 us
    pallas_call x1, Pallas kernels: 31.3 us -> 29.6 us  [body(): pl.pallas_call(strip_kernel, out_shape=jax.ShapeDtypeStruct((tiles,) + st...]
  transfers between devices with their start and end apart: 3 -> 4, of which waited for: 1 -> 2; matrix products, arithmetic and copies ran while one was open for 5% -> 5% of each run, Pallas kernels for 35% -> 34%
where the time goes in v4:
time: 170 us; the launch traced here: 169 us
  Pallas kernels  70.7 us (42%)
  waiting for transfers between devices  61.7 us (36%)
  between operations  17.5 us (10%)
  local copies, waits for them, and re-layouts  12.3 us (7%)
  starting transfers between devices  4.41 us (3%)
  other arithmetic  2.61 us (2%)
    all_gather x2, waiting for transfers between devices, body(): lax.all_gather(share, ('tile', 'slab'), axis=0)  61.7 us
    pallas_call x1, Pallas kernels, body(): pl.pallas_call(strip_kernel, out_shape=jax.ShapeDtypeStruct((tiles,) + st...  29.6 us
    pallas_call x1, Pallas kernels, body(): pl.pallas_call(expand_kernel, grid=(count,), out_shape=(jax.ShapeDtypeStr...  15.3 us
    pallas_call x1, Pallas kernels, body(): pl.pallas_call(shrink_kernel, grid=(count,), out_shape=jax.ShapeDtypeStru...  13.6 us
    pallas_call x1, Pallas kernels, body(): pl.pallas_call(band_kernel, out_shape=(jax.ShapeDtypeStruct((planes, rows...  12.2 us
    unnamed x24, local copies, waits for them, and re-layouts  4.64 us
  transfers between devices with their start and end apart: 4, of which 2 were waited for; matrix products, arithmetic and copies ran while one was open for 5% of the time, Pallas kernels for 34%

profile of v4, /device:TPU:0, one launch (start us, length us, event | category | flops | bytes accessed | tf_op | source)
XLA Modules:
  0.0 169.2 jit_solution(8499452234127786340)
XLA Ops:
  7.2 0.0 copy-start
  7.2 0.0 copy-start.6
  7.2 0.0 copy-start.8
  7.2 0.0 copy-start.9
  7.2 0.0 all-gather.5.cloned.1.call-start
  7.3 1.1 dynamic-slice_bitcast_fusion.2
  8.4 0.0 copy-done
  8.5 0.0 copy-start.7
  8.5 0.7 copy-done.7
  9.2 0.0 all-gather.5.cloned.1.call-update
  9.2 0.0 all-gather.7.cloned.1.call-start
  9.2 0.9 dynamic-slice_bitcast_fusion
  10.2 1.4 fusion.10
  11.5 0.0 all-gather.7.cloned.1.call-update
  11.6 0.0 copy-done.6
  11.6 1.3 collective-permute-start.1
  12.9 3.0 %collective-permute-start = (bf16[4,64,256]{2,1,0:T(8,128)(2,1)S(1)}, bf16[4,64,256]{2,1,0:T(8,128)(2,1)S(1)}, u32[]{:S(2)}, u32[]{:S(2)}) collective-permute-start(bf16[4,64,256]{2,1,0:T(8,128)(2,1)S(1)} %get-tuple-element.12), channel_id=1, source_target_pairs={{0,1},{1,2},{2,3},{4,5},{5,6},{6,7},{8,9},{9,10},{10,11},{12,13},{... | collective-permute-start | bytes 393224 | tf_op jit(solution)/shard_map/ppermute | solution.py:208
  16.0 0.1 add_convert_fusion.flags_ref
  16.0 0.0 copy-done.8
  16.0 0.6 dynamic_slice.26
  17.9 0.0 copy-done.9
  17.9 0.6 dynamic_slice.28
  20.5 0.1 select_add_fusion.band_ref
  20.6 0.0 collective-permute-done.1
  20.6 0.0 collective-permute-done
  20.6 0.2 pad_maximum_fusion.1
  20.7 1.6 slice.50
  22.4 0.1 slice.49
  22.5 0.9 reshape.37.own_ref
  23.3 29.6 %strips.1 = bf16[8,24,16,128]{3,2,1,0:T(8,128)(2,1)} custom-call(bf16[24,16,128]{2,1,0:T(8,128)(2,1)} %reshape.37.own_ref), custom_call_target="tpu_custom_call" | custom-call | bytes 40000000 | tf_op jit(solution)/shard_map/strips/pallas_call | solution.py:215
  53.0 0.9 constant_dynamic-slice_fusion
  53.9 0.2 reshape.38
  54.1 0.0 copy-start.5
  54.1 0.4 fusion
  54.5 1.0 copy-done.5
  55.5 0.5 pad_maximum_fusion.joined_ref
  56.0 0.0 copy-start.1
  56.0 0.0 copy-start.2
  56.0 12.2 %band.1 = (f32[16,64,256]{2,1,0:T(8,128)}, bf16[256,32,128]{2,1,0:T(8,128)(2,1)S(1)}) custom-call(f32[2]{0:T(128)S(1)} %add_convert_fusion.flags_ref, f32[24,64,256]{2,1,0:T(8,128)S(1)} %pad_maximum_fusion.joined_ref, f32[256,256]{1,0:T(8,128)S(1)} %select_add_fusion.band_ref), custom_call_target="tpu_custom_call" | custom-call | flops 1000000000 | bytes 6000000 | tf_op jit(solution)/shard_map/band/pallas_call | solution.py:251
  68.2 1.3 copy-done.3
  69.5 14.1 %all-gather.5.cloned.1.call-done = bf16[12288,256]{1,0:T(8,128)(2,1)} async-done(((bf16[384,256]{1,0:T(8,128)(2,1)}), bf16[12288,256]{1,0:T(8,128)(2,1)}) %all-gather.5.cloned.1.call-update) | async-done | bytes 6291472 | tf_op jit(solution)/shard_map/all_gather | solution.py:230
  83.6 0.0 copy-done.1
  83.6 0.0 copy-done.2
  83.6 1.6 copy-done.4
  85.2 15.3 %expand.1 = (bf16[16,256,256]{2,1,0:T(8,128)(2,1)S(1)}, bf16[16,256,1024]{2,1,0:T(8,128)(2,1)}) custom-call(s32[16]{0:T(128)S(1)} %copy-done.2, s32[16]{0:T(128)S(1)} %bitcast.30, bf16[256,32,128]{2,1,0:T(8,128)(2,1)S(1)} %copy-done.4, bf16[8,4,384,256]{3,2,1,0:T(8,128)(2,1)} %bitcast.38), custom_call_target="tpu_custom_call" | custom-call | flops 3200000000 | bytes 20000000 | tf_op jit(solution)/shard_map/expand/pallas_call | solution.py:276
  100.5 47.5 %all-gather.7.cloned.1.call-done = bf16[8704,256]{1,0:T(8,128)(2,1)} async-done(((bf16[272,256]{1,0:T(8,128)(2,1)}), bf16[8704,256]{1,0:T(8,128)(2,1)}) %all-gather.7.cloned.1.call-update) | async-done | bytes 4456464 | tf_op jit(solution)/shard_map/all_gather | solution.py:230
  148.0 13.6 %shrink.1 = f32[16,8,128]{2,1,0:T(8,128)S(1)} custom-call(s32[16]{0:T(128)S(1)} %bitcast.31, bf16[16,256,256]{2,1,0:T(8,128)(2,1)S(1)} %get-tuple-element.8.hidden_ref, bf16[16,256,1024]{2,1,0:T(8,128)(2,1)} %get-tuple-element.9.expanded_ref, bf16[8,4,272,256]{3,2,1,0:T(8,128)(2,1)} %bitcast.32), custom_call_target="tpu_custom_call" | custom-call | flops 2100000000 | bytes 15000000 | tf_op jit(solution)/shard_map/shrink/pallas_call | solution.py:289
  161.7 0.7 copy.21
  (11 shorter events, 0.1 us)
Async XLA Ops:
  7.2 1.2 copy-start
  7.2 4.4 %copy-start.6 = (bf16[1,16,64,256]{3,2,1,0:T(8,128)(2,1)S(1)}, bf16[1,16,64,256]{3,2,1,0:T(8,128)(2,1)}, u32[]{:S(2)}) copy-start(bf16[1,16,64,256]{3,2,1,0:T(8,128)(2,1)} %param.9) | copy-start | bytes 1572868
  7.2 8.9 %copy-start.8 = (s32[8]{0:T(128)S(1)}, s32[8]{0:T(128)}, u32[]{:S(2)}) copy-start(s32[8]{0:T(128)} %param.10) | copy-start | bytes 100
  7.2 10.7 %copy-start.9 = (s32[8]{0:T(128)S(1)}, s32[8]{0:T(128)}, u32[]{:S(2)}) copy-start(s32[8]{0:T(128)} %param.11) | copy-start | bytes 100
  7.2 76.4 %all-gather.5.cloned.1.call-start = ((), (), s32[]{:S(2)}) async-start(), calls=%async_computation | async-start | bytes 6488064 | tf_op jit(solution)/shard_map/all_gather | solution.py:230
  8.5 0.7 copy-start.7
  9.2 138.8 %all-gather.7.cloned.1.call-start = ((), (), s32[]{:S(2)}) async-start(), calls=%async_computation.1 | async-start | bytes 4595712 | tf_op jit(solution)/shard_map/all_gather | solution.py:230
  11.6 9.0 %collective-permute-start.1 = (bf16[4,64,256]{2,1,0:T(8,128)(2,1)S(1)}, bf16[4,64,256]{2,1,0:T(8,128)(2,1)S(1)}, u32[]{:S(2)}, u32[]{:S(2)}) collective-permute-start(bf16[4,64,256]{2,1,0:T(8,128)(2,1)S(1)} %get-tuple-element.13), channel_id=1, source_target_pairs={{1,0},{2,1},{3,2},{5,4},{6,5},{7,6},{9,8},{10,9},{11,10},{13,12},{... | collective-permute-start | bytes 393224 | tf_op jit(solution)/shard_map/ppermute | solution.py:209
  12.9 7.7 %collective-permute-start = (bf16[4,64,256]{2,1,0:T(8,128)(2,1)S(1)}, bf16[4,64,256]{2,1,0:T(8,128)(2,1)S(1)}, u32[]{:S(2)}, u32[]{:S(2)}) collective-permute-start(bf16[4,64,256]{2,1,0:T(8,128)(2,1)S(1)} %get-tuple-element.12), channel_id=1, source_target_pairs={{0,1},{1,2},{2,3},{4,5},{5,6},{6,7},{8,9},{9,10},{10,11},{12,13},{... | collective-permute-start | bytes 393224 | tf_op jit(solution)/shard_map/ppermute | solution.py:208
  54.1 1.4 copy-start.5
  56.0 27.6 %copy-start.1 = (s32[16,1]{0,1:T(1,128)S(1)}, s32[16,1]{0,1:T(1,128)}, u32[]{:S(2)}) copy-start(s32[16,1]{0,1:T(1,128)} %param.13) | copy-start | bytes 196
  56.0 27.6 %copy-start.2 = (s32[16]{0:T(128)S(1)}, s32[16]{0:T(128)}, u32[]{:S(2)}) copy-start(s32[16]{0:T(128)} %starts_ref.1) | copy-start | bytes 196
  68.2 1.3 copy-start.3
  83.6 1.6 copy-start.4
Sparse Core Ops, SparseCore 0:
  10.9 72.6 all-gather.4
  86.5 61.5 all-gather.6

commit v5 on v3

--- a/solution.py
+++ b/solution.py
@@ -141,7 +141,7 @@
     def rows_of(route, first, length):
         return jnp.concatenate([weights_ref[route, s, first : first + length] for s in range(slabs)], axis=0)
 
-    @pl.loop(0, out_ref.shape[0], unroll=2)
+    @pl.loop(0, out_ref.shape[0], unroll=4)
     def _(i):
         start = starts_ref[i]
         route = routes_ref[i]

time: 126 us -> 124 us (0.984)
  Pallas kernels: 59.1 us -> 57.4 us
    pallas_call x1, Pallas kernels: 15.6 us -> 13.9 us  [body(): pl.pallas_call(classify_kernel, out_shape=jax.ShapeDtypeStruct((count, 8,...]
where the time goes in v5:
time: 124 us
  Pallas kernels  57.4 us (46%)
  waiting for transfers between devices  33.5 us (27%)
  between operations  17.4 us (14%)
  local copies, waits for them, and re-layouts  10.1 us (8%)
  starting transfers between devices  4.37 us (4%)
  other arithmetic  1.25 us (1%)
    all_gather x1, waiting for transfers between devices, body(): weights = lax.all_gather(share, ('tile', 'slab'), axis=0)  33.5 us
    pallas_call x1, Pallas kernels, body(): pl.pallas_call(strip_kernel, out_shape=jax.ShapeDtypeStruct((tiles,) + st...  31.3 us
    pallas_call x1, Pallas kernels, body(): pl.pallas_call(classify_kernel, out_shape=jax.ShapeDtypeStruct((count, 8,...  13.9 us
    pallas_call x1, Pallas kernels, body(): pl.pallas_call(band_kernel, out_shape=(jax.ShapeDtypeStruct((planes, rows...  12.2 us
    ppermute x1, starting transfers between devices, body(): before = lax.ppermute(raw[planes - HALO:], 'slab', up)  3.04 us
    unnamed x22, local copies, waits for them, and re-layouts  2.72 us
  transfers between devices with their start and end apart: 3, of which 1 were waited for; matrix products, arithmetic and copies ran while one was open for 5% of the time, Pallas kernels for 35%

profile of v5, /device:TPU:0, one launch (start us, length us, event | category | flops | bytes accessed | tf_op | source)
XLA Modules:
  0.0 124.1 jit_solution(5854219988778901739)
XLA Ops:
  7.2 0.0 copy-start
  7.2 0.0 copy-start.4
  7.2 0.0 copy-start.6
  7.2 0.0 copy-start.7
  7.2 0.0 all-gather.3.cloned.1.call-start
  7.3 1.1 dynamic-slice_bitcast_fusion.1
  8.4 0.0 copy-done
  8.5 0.9 bitcast_dynamic-update-slice_fusion
  9.4 0.7 constant_dynamic-update-slice_fusion
  10.1 0.0 copy-start.5
  10.1 0.7 copy-done.5
  10.9 0.0 all-gather.3.cloned.1.call-update
  10.9 0.0 copy-done.4
  10.9 1.3 %collective-permute-start.1 = (bf16[4,64,256]{2,1,0:T(8,128)(2,1)S(1)}, bf16[4,64,256]{2,1,0:T(8,128)(2,1)S(1)}, u32[]{:S(2)}, u32[]{:S(2)}) collective-permute-start(bf16[4,64,256]{2,1,0:T(8,128)(2,1)S(1)} %get-tuple-element.9), channel_id=1, source_target_pairs={{1,0},{2,1},{3,2},{5,4},{6,5},{7,6},{9,8},{10,9},{11,10},{13,12},{... | collective-permute-start | bytes 393224 | tf_op jit(solution)/shard_map/ppermute | solution.py:205
  12.2 3.0 %collective-permute-start = (bf16[4,64,256]{2,1,0:T(8,128)(2,1)S(1)}, bf16[4,64,256]{2,1,0:T(8,128)(2,1)S(1)}, u32[]{:S(2)}, u32[]{:S(2)}) collective-permute-start(bf16[4,64,256]{2,1,0:T(8,128)(2,1)S(1)} %get-tuple-element.8), channel_id=1, source_target_pairs={{0,1},{1,2},{2,3},{4,5},{5,6},{6,7},{8,9},{9,10},{10,11},{12,13},{... | collective-permute-start | bytes 393224 | tf_op jit(solution)/shard_map/ppermute | solution.py:204
  15.3 0.1 add_convert_fusion.flags_ref
  15.4 0.0 copy-done.6
  15.4 0.6 dynamic_slice.26
  17.2 0.0 copy-done.7
  17.2 0.6 dynamic_slice.28
  19.7 0.1 select_add_fusion.band_ref
  19.8 0.0 collective-permute-done.1
  19.8 0.0 collective-permute-done
  19.9 0.2 pad_maximum_fusion.1
  20.0 1.6 %slice.50 = f32[24,64,224]{2,1,0:T(8,128)} slice(f32[24,64,256]{2,1,0:T(8,128)S(1)} %get-tuple-element.7), slice={[0:24], [0:64], [32:256]} | slice | bytes 2752512 | tf_op jit(solution)/shard_map/slice | solution.py:236
  21.6 0.1 slice.49
  21.7 0.9 reshape.34.own_ref
  22.6 31.3 %strips.1 = bf16[8,24,16,128]{3,2,1,0:T(8,128)(2,1)} custom-call(bf16[24,16,128]{2,1,0:T(8,128)(2,1)} %reshape.34.own_ref), custom_call_target="tpu_custom_call" | custom-call | bytes 40000000 | tf_op jit(solution)/shard_map/strips/pallas_call | solution.py:211
  53.9 0.9 constant_dynamic-slice_fusion
  54.8 0.2 reshape.35
  55.0 0.0 copy-start.3
  55.0 0.4 fusion
  55.4 1.0 copy-done.3
  56.4 0.5 pad_maximum_fusion.joined_ref
  56.9 0.0 copy-start.1
  56.9 0.0 copy-start.2
  56.9 12.2 %band.1 = (f32[16,64,256]{2,1,0:T(8,128)}, bf16[256,32,128]{2,1,0:T(8,128)(2,1)S(1)}) custom-call(f32[2]{0:T(128)S(1)} %add_convert_fusion.flags_ref, f32[24,64,256]{2,1,0:T(8,128)S(1)} %pad_maximum_fusion.joined_ref, f32[256,256]{1,0:T(8,128)S(1)} %select_add_fusion.band_ref), custom_call_target="tpu_custom_call" | custom-call | flops 1000000000 | bytes 6000000 | tf_op jit(solution)/shard_map/band/pallas_call | solution.py:246
  69.1 33.5 %all-gather.3.cloned.1.call-done = bf16[20992,256]{1,0:T(8,128)(2,1)} async-done(((bf16[656,256]{1,0:T(8,128)(2,1)}), bf16[20992,256]{1,0:T(8,128)(2,1)}) %all-gather.3.cloned.1.call-update) | async-done | bytes 10747920 | tf_op jit(solution)/shard_map/all_gather | solution.py:225
  102.6 0.0 copy-done.1
  102.6 0.0 copy-done.2
  102.6 13.9 %classify.1 = f32[16,8,128]{2,1,0:T(8,128)S(1)} custom-call(s32[16]{0:T(128)S(1)} %copy-done.1, s32[16]{0:T(128)S(1)} %bitcast.29, bf16[256,32,128]{2,1,0:T(8,128)(2,1)S(1)} %get-tuple-element.5.table_ref, bf16[8,4,656,256]{3,2,1,0:T(8,128)(2,1)} %bitcast.35), custom_call_target="tpu_custom_call" | custom-call | flops 5400000000 | bytes 13000000 | tf_op jit(solution)/shard_map/classify/pallas_call | solution.py:265
  116.5 0.7 copy.21
  (9 shorter events, 0.1 us)
Async XLA Ops:
  7.2 1.2 copy-start
  7.2 3.7 %copy-start.4 = (bf16[1,16,64,256]{3,2,1,0:T(8,128)(2,1)S(1)}, bf16[1,16,64,256]{3,2,1,0:T(8,128)(2,1)}, u32[]{:S(2)}) copy-start(bf16[1,16,64,256]{3,2,1,0:T(8,128)(2,1)} %param.9) | copy-start | bytes 1572868
  7.2 8.2 %copy-start.6 = (s32[8]{0:T(128)S(1)}, s32[8]{0:T(128)}, u32[]{:S(2)}) copy-start(s32[8]{0:T(128)} %param.10) | copy-start | bytes 100
  7.2 10.0 %copy-start.7 = (s32[8]{0:T(128)S(1)}, s32[8]{0:T(128)}, u32[]{:S(2)}) copy-start(s32[8]{0:T(128)} %param.11) | copy-start | bytes 100
  7.2 95.4 %all-gather.3.cloned.1.call-start = ((), (), s32[]{:S(2)}) async-start(), calls=%async_computation | async-start | bytes 11083776 | tf_op jit(solution)/shard_map/all_gather | solution.py:225
  10.1 0.7 copy-start.5
  10.9 8.9 %collective-permute-start.1 = (bf16[4,64,256]{2,1,0:T(8,128)(2,1)S(1)}, bf16[4,64,256]{2,1,0:T(8,128)(2,1)S(1)}, u32[]{:S(2)}, u32[]{:S(2)}) collective-permute-start(bf16[4,64,256]{2,1,0:T(8,128)(2,1)S(1)} %get-tuple-element.9), channel_id=1, source_target_pairs={{1,0},{2,1},{3,2},{5,4},{6,5},{7,6},{9,8},{10,9},{11,10},{13,12},{... | collective-permute-start | bytes 393224 | tf_op jit(solution)/shard_map/ppermute | solution.py:205
  12.2 7.6 %collective-permute-start = (bf16[4,64,256]{2,1,0:T(8,128)(2,1)S(1)}, bf16[4,64,256]{2,1,0:T(8,128)(2,1)S(1)}, u32[]{:S(2)}, u32[]{:S(2)}) collective-permute-start(bf16[4,64,256]{2,1,0:T(8,128)(2,1)S(1)} %get-tuple-element.8), channel_id=1, source_target_pairs={{0,1},{1,2},{2,3},{4,5},{5,6},{6,7},{8,9},{9,10},{10,11},{12,13},{... | collective-permute-start | bytes 393224 | tf_op jit(solution)/shard_map/ppermute | solution.py:204
  55.0 1.4 %copy-start.3 = (f32[24,64,224]{2,1,0:T(8,128)S(1)}, f32[24,64,224]{2,1,0:T(8,128)}, u32[]{:S(2)}) copy-start(f32[24,64,224]{2,1,0:T(8,128)} %slice.50) | copy-start | bytes 4128772
  56.9 45.7 %copy-start.1 = (s32[16]{0:T(128)S(1)}, s32[16]{0:T(128)}, u32[]{:S(2)}) copy-start(s32[16]{0:T(128)} %starts_ref.1) | copy-start | bytes 196
  56.9 45.7 %copy-start.2 = (s32[16,1]{0,1:T(1,128)S(1)}, s32[16,1]{0,1:T(1,128)}, u32[]{:S(2)}) copy-start(s32[16,1]{0,1:T(1,128)} %param.13) | copy-start | bytes 196
Sparse Core Ops, SparseCore 0:
  11.0 91.5 all-gather.2
